TPU v7x, 128 devices: a whole 4x4x4 slice. The times are simulated.
128 devices in a mesh: gx: 32 (over x, y_hi, z), gy: 4 (over y_lo, core).
Axes of the slice: x: 4, y: 4 (y_hi: 2, y_lo: 2; y = y_hi * 2 + y_lo), z: 4, core: 2. Of those that a mesh axis runs over, the one named last changes fastest.
Arguments:
- misfit: float32 [2, 16, 1024, 1024], P(None, None, 'gx', 'gy'), may hold values from -6 to 6
- viscosity: float32 [16, 1024, 1024], P(None, 'gx', 'gy'), may hold values from 0.1 to 10
- friction: float32 [1024, 1024], P('gx', 'gy'), may hold values from 0.5 to 50
- ice_mask: int32 [1024, 1024], P('gx', 'gy'), may hold values 0 or 1
- grounded: int32 [1024, 1024], P('gx', 'gy'), may hold values 0 or 1
Outputs:
- adjoint_velocity: float32 [2, 16, 1024, 1024], P(None, None, 'gx', 'gy')
All inputs are finite; a program needn't handle non-finite values. No bound on the sum of `ice_mask` or of `grounded` on one device may be relied on, other than what follows from the above.
Results may differ from a plain program's by a relative error of at most 0.00002.
Values sent between devices are 32-bit elements; how exact they have to be, the bound alone decides.
A program may use at most 128 MiB of HBM per device.

v0:
```python
import jax
import jax.numpy as jnp
from jax import lax
from jax.sharding import PartitionSpec as P

LEVELS = 4
SWEEPS = 2
COARSE_ITERS = 20


OMEGA = 0.6
ZWEIGHT = 4.0
CROSS = 0.75


def padded_2(cells, sides, width):
    for axis, dim in sides:
        count = lax.axis_size(axis)
        ends = count - 1
        head = lax.slice_in_dim(cells, 0, width, axis=dim)
        tail = lax.slice_in_dim(cells, cells.shape[dim] - width, cells.shape[dim], axis=dim)
        cells = jnp.concatenate(
            [
                lax.ppermute(tail, axis, [(i, (i + 1) % count) for i in range(ends)]),
                cells,
                lax.ppermute(head, axis, [((i + 1) % count, i) for i in range(ends)]),
            ],
            axis=dim,
        )
    return cells


def apply_operator(padded, coef_pad, horizontal):
    layers = padded.shape[1]
    viscous = coef_pad[:layers]
    ice_share = coef_pad[layers, 1:-1, 1:-1]
    drag_term = coef_pad[layers + 1, 1:-1, 1:-1]
    centre = viscous[:, 1:-1, 1:-1]
    east_face = 0.5 * (centre + viscous[:, 2:, 1:-1])
    west_face = 0.5 * (centre + viscous[:, :-2, 1:-1])
    north_face = 0.5 * (centre + viscous[:, 1:-1, 2:])
    south_face = 0.5 * (centre + viscous[:, 1:-1, :-2])
    vertical = ZWEIGHT * 0.5 * (centre[1:] + centre[:-1])
    layer_index = lax.broadcasted_iota(jnp.int32, centre.shape, 0)
    bottom = jnp.where(layer_index == 0, drag_term, jnp.zeros_like(centre))
    vert_diag = jnp.pad(vertical, ((1, 0), (0, 0), (0, 0))) + jnp.pad(
        vertical, ((0, 1), (0, 0), (0, 0))
    )
    images = []
    diagonals = []
    for component, (x_weight, y_weight) in enumerate(((4.0, 1.0), (1.0, 4.0))):
        field = padded[component]
        middle = field[:, 1:-1, 1:-1]
        lateral = x_weight * (
            east_face * (middle - field[:, 2:, 1:-1]) + west_face * (middle - field[:, :-2, 1:-1])
        )
        lateral = lateral + y_weight * (
            north_face * (middle - field[:, 1:-1, 2:]) + south_face * (middle - field[:, 1:-1, :-2])
        )
        fluxes = vertical * (middle[1:] - middle[:-1])
        column = jnp.pad(fluxes, ((1, 0), (0, 0), (0, 0))) - jnp.pad(
            fluxes, ((0, 1), (0, 0), (0, 0))
        )
        other = padded[1 - component]
        mixed = other[:, 2:, 2:] - other[:, 2:, :-2] - other[:, :-2, 2:] + other[:, :-2, :-2]
        flow = horizontal * (lateral - CROSS * centre * mixed) + column + bottom * middle
        images.append(ice_share * flow + (1.0 - ice_share) * middle)
        lateral_diag = x_weight * (east_face + west_face) + y_weight * (north_face + south_face)
        diagonals.append(
            ice_share * (horizontal * lateral_diag + vert_diag + bottom) + (1.0 - ice_share)
        )
    return (jnp.stack(images), jnp.stack(diagonals))


def jacobi_update(inside, target, padded, coef_pad, horizontal):
    image, diagonal = apply_operator(padded, coef_pad, horizontal)
    return inside + OMEGA * (target - image) / diagonal


def strip_rim(array, width):
    if width == 0:
        return array
    return array[..., width:-width, width:-width]


def restrict(array):
    shape = array.shape
    blocks = array.reshape(shape[:-2] + (shape[-2] // 2, 2, shape[-1] // 2, 2))
    return jnp.mean(blocks, axis=(-3, -1))


def prolong(array):
    return jnp.repeat(jnp.repeat(array, 2, axis=-2), 2, axis=-1)


def stack_level(target, coefs):
    layers = target.shape[1]
    return jnp.concatenate([target.reshape((2 * layers,) + target.shape[2:]), coefs], 0)


def split_level(padded, layers):
    return (padded[: 2 * layers].reshape((2, layers) + padded.shape[1:]), padded[2 * layers :])


def level_data(target, coefs, width):
    padded = padded_2(stack_level(target, coefs), (("gx", 1), ("gy", 2)), width)
    return split_level(padded, target.shape[1])


def smooth(solution, target_pad, coef_pad, width, horizontal):
    for sweep in range(SWEEPS):
        padded = padded_2(solution, (("gx", 2), ("gy", 3)), 1)
        solution = jacobi_update(
            solution,
            strip_rim(target_pad, width),
            padded,
            strip_rim(coef_pad, width - 1),
            horizontal,
        )
    return solution


def coarse_solve(target, coefs, horizontal):
    layers = target.shape[1]
    padded = padded_2(stack_level(target, coefs), (("gx", 1), ("gy", 2)), 1)
    target_pad, coef_pad = split_level(padded, layers)
    inner_target = strip_rim(target_pad, 1)

    def spread_step(iteration, current):
        beside_all = padded_2(current, (("gx", 2), ("gy", 3)), 1)
        return jacobi_update(current, inner_target, beside_all, coef_pad, horizontal)

    return lax.fori_loop(0, COARSE_ITERS, spread_step, jnp.zeros_like(target))


def cycle(level, target, coefs):
    horizontal = 0.25**level
    if level == LEVELS - 1:
        return coarse_solve(target, coefs, horizontal)
    width = 1
    target_pad, coef_pad = level_data(target, coefs, width)
    solution = smooth(jnp.zeros_like(target), target_pad, coef_pad, width, horizontal)
    padded = padded_2(solution, (("gx", 2), ("gy", 3)), 1)
    image, diagonal = apply_operator(padded, strip_rim(coef_pad, width - 1), horizontal)
    remainder = strip_rim(target_pad, width) - image
    correction = cycle(level + 1, restrict(remainder), restrict(coefs))
    solution = solution + prolong(correction)
    return smooth(solution, target_pad, coef_pad, width, horizontal)


def per_device(misfit, viscosity, friction, ice_mask, grounded):
    ice_share = ice_mask.astype(jnp.float32)
    drag_term = friction * grounded.astype(jnp.float32)
    coefs = jnp.concatenate([viscosity, ice_share[None], drag_term[None]], 0)
    return cycle(0, misfit * ice_share, coefs)


def solution(mesh):
    placed = (
        P(None, None, "gx", "gy"),
        P(None, "gx", "gy"),
        P("gx", "gy"),
        P("gx", "gy"),
        P("gx", "gy"),
    )
    return jax.shard_map(
        per_device, mesh=mesh, in_specs=placed, out_specs=P(None, None, "gx", "gy"), check_vma=False
    )
```

profile of v0, /device:TPU:5, one launch (start us, length us, event | category | flops | bytes accessed | tf_op | source)
XLA Modules:
  0.0 1211.4 jit_solution(16778615599544277127)
XLA Ops:
  0.6 8.3 collective-permute-start.9
  11.4 7.9 collective-permute-start.41
  23.4 7.6 concatenate.262
  31.0 7.6 concatenate.261
  41.2 11.6 maximum_reduce_fusion
  63.7 7.9 collective-permute-start.25
  75.0 7.9 collective-permute-start.5
  141.1 8.8 collective-permute-start.13
  153.2 5.8 collective-permute-done.12
  214.7 6.0 copy.917
  220.7 10.9 reduce_sum.54
  237.4 8.2 collective-permute-start.21
  271.3 9.2 collective-permute-start.29
  294.6 8.1 collective-permute-start.33
  327.1 9.0 collective-permute-start.37
  338.2 7.0 collective-permute-done.36
  364.3 5.6 collective-permute-done.44
  371.9 5.9 collective-permute-start.46
  396.1 5.5 collective-permute-start.50
  453.9 563.4 %while.13 = (s32[]{:T(128)}, f32[2,16,4,32]{3,2,1,0:T(4,128)}, f32[18,6,34]{2,1,0:T(8,128)}, f32[16,4,32]{2,1,0:T(4,128)S(1)}, f32[16,4,32]{2,1,0:T(4,128)}, /*i...) while((s32[]{:T(128)}, f32[2,16,4,32]{3,2,1,0:T(4,128)}, ...), condition=%wide.region_7.8_spmd.clone, body=%wide.region_6.7_spmd.clone.sunk | while | flops 252947 | bytes 1027220 | solution.py:133
  551.5 5.5 collective-permute-start.3
  636.3 5.5 collective-permute-start.3
  721.1 5.5 collective-permute-start.3
  1029.4 5.6 collective-permute-done.56
  1051.4 5.6 collective-permute-done.60
  1059.1 5.5 collective-permute-start.62
  1078.5 7.9 collective-permute-start.65
  1089.3 5.8 collective-permute-start.66
  1103.2 9.2 collective-permute-start.69
  1140.0 9.0 collective-permute-start.73
  1151.0 7.2 collective-permute-done.72
  1184.0 5.6 collective-permute-done.76
  (1470 shorter events, 977.4 us)
Async XLA Ops:
  0.6 84.3 %collective-permute-start.9 = (f32[2,16,1,256]{3,1,2,0:T(8,128)}, f32[2,16,1,256]{3,1,2,0:T(8,128)}, u32[]{:S(2)}, u32[]{:S(2)}) collective-permute-start(f32[2,16,1,256]{3,1,2,0:T(8,128)} %broadcast.323), channel_id=1, source_target_pairs={{4,0},{8,4},{12,8},{16,12},{20,16},{24,20},{28,24},{32,28},{36,32}... | collective-permute-start | bytes 98312 | tf_op jit(solution)/shard_map/ppermute | solution.py:26
  8.9 76.0 %collective-permute-start.8 = (f32[2,16,1,256]{3,1,2,0:T(8,128)}, f32[2,16,1,256]{3,1,2,0:T(8,128)}, u32[]{:S(2)}, u32[]{:S(2)}) collective-permute-start(f32[2,16,1,256]{3,1,2,0:T(8,128)} %broadcast.323), channel_id=1, source_target_pairs={{0,4},{4,8},{8,12},{12,16},{16,20},{20,24},{24,28},{28,32},{32,36}... | collective-permute-start | bytes 98312 | tf_op jit(solution)/shard_map/ppermute | solution.py:24
  11.4 60.1 %collective-permute-start.41 = (f32[2,16,1,64]{3,1,2,0:T(8,128)}, f32[2,16,1,64]{3,1,2,0:T(8,128)}, u32[]{:S(2)}, u32[]{:S(2)}) collective-permute-start(f32[2,16,1,64]{3,1,2,0:T(8,128)} %broadcast.341), channel_id=1, source_target_pairs={{4,0},{8,4},{12,8},{16,12},{20,16},{24,20},{28,24},{32,28},{36,32}... | collective-permute-start | bytes 24584 | tf_op jit(solution)/shard_map/ppermute | solution.py:26
  19.3 54.2 %collective-permute-start.40 = (f32[2,16,1,64]{3,1,2,0:T(8,128)}, f32[2,16,1,64]{3,1,2,0:T(8,128)}, u32[]{:S(2)}, u32[]{:S(2)}) collective-permute-start(f32[2,16,1,64]{3,1,2,0:T(8,128)} %broadcast.341), channel_id=1, source_target_pairs={{0,4},{4,8},{8,12},{12,16},{16,20},{20,24},{24,28},{28,32},{32,36}... | collective-permute-start | bytes 24584 | tf_op jit(solution)/shard_map/ppermute | solution.py:24
  63.7 19.2 %collective-permute-start.25 = (f32[2,16,1,128]{3,1,2,0:T(8,128)S(1)}, f32[2,16,1,128]{3,1,2,0:T(8,128)S(1)}, u32[]{:S(2)}, u32[]{:S(2)}) collective-permute-start(f32[2,16,1,128]{3,1,2,0:T(8,128)S(1)} %broadcast.332), channel_id=1, source_target_pairs={{4,0},{8,4},{12,8},{16,12},{20,16},{24,20},{28,24},{32,28},{36,32}... | collective-permute-start | bytes 49160 | tf_op jit(solution)/shard_map/ppermute | solution.py:26
  71.5 13.3 %collective-permute-start.24 = (f32[2,16,1,128]{3,1,2,0:T(8,128)S(1)}, f32[2,16,1,128]{3,1,2,0:T(8,128)S(1)}, u32[]{:S(2)}, u32[]{:S(2)}) collective-permute-start(f32[2,16,1,128]{3,1,2,0:T(8,128)S(1)} %broadcast.332), channel_id=1, source_target_pairs={{0,4},{4,8},{8,12},{12,16},{16,20},{20,24},{24,28},{28,32},{32,36}... | collective-permute-start | bytes 49160 | tf_op jit(solution)/shard_map/ppermute | solution.py:24
  75.0 32.9 %collective-permute-start.5 = (f32[50,1,256]{2,1,0:T(1,128)}, f32[50,1,256]{2,1,0:T(1,128)}, u32[]{:S(2)}, u32[]{:S(2)}) collective-permute-start(f32[50,1,256]{2,1,0:T(1,128)} %get-tuple-element.235), channel_id=1, source_target_pairs={{4,0},{8,4},{12,8},{16,12},{20,16},{24,20},{28,24},{32,28},{36,32}... | collective-permute-start | bytes 153608 | tf_op jit(solution)/shard_map/ppermute | solution.py:26
  82.9 26.0 %collective-permute-start.4 = (f32[50,1,256]{2,1,0:T(1,128)}, f32[50,1,256]{2,1,0:T(1,128)}, u32[]{:S(2)}, u32[]{:S(2)}) collective-permute-start(f32[50,1,256]{2,1,0:T(1,128)} %get-tuple-element.234), channel_id=1, source_target_pairs={{0,4},{4,8},{8,12},{12,16},{16,20},{20,24},{24,28},{28,32},{32,36}... | collective-permute-start | bytes 153608 | tf_op jit(solution)/shard_map/ppermute | solution.py:24
  88.5 11.6 collective-permute-start.11
  97.9 53.9 %collective-permute-start.27 = (f32[2,16,18,1]{3,1,2,0:T(8,128)}, f32[2,16,18,1]{3,1,2,0:T(8,128)}, u32[]{:S(2)}, u32[]{:S(2)}) collective-permute-start(f32[2,16,18,1]{3,1,2,0:T(8,128)} %get-tuple-element.289), channel_id=1, source_target_pairs={{1,0},{2,1},{3,2},{5,4},{6,5},{7,6},{9,8},{10,9},{11,10},{13,12},{... | collective-permute-start | bytes 6920 | tf_op jit(solution)/shard_map/ppermute | solution.py:26
  100.4 51.4 %collective-permute-start.26 = (f32[2,16,18,1]{3,1,2,0:T(8,128)}, f32[2,16,18,1]{3,1,2,0:T(8,128)}, u32[]{:S(2)}, u32[]{:S(2)}) collective-permute-start(f32[2,16,18,1]{3,1,2,0:T(8,128)} %get-tuple-element.288), channel_id=1, source_target_pairs={{0,1},{1,2},{2,3},{4,5},{5,6},{6,7},{8,9},{9,10},{10,11},{12,13},{... | collective-permute-start | bytes 6920 | tf_op jit(solution)/shard_map/ppermute | solution.py:24
  115.5 13.6 %collective-permute-start.7 = (f32[50,34,1]{0,2,1:T(1,128)S(1)}, f32[50,34,1]{0,2,1:T(1,128)S(1)}, u32[]{:S(2)}, u32[]{:S(2)}) collective-permute-start(f32[50,34,1]{0,2,1:T(1,128)S(1)} %get-tuple-element.223), channel_id=1, source_target_pairs={{1,0},{2,1},{3,2},{5,4},{6,5},{7,6},{9,8},{10,9},{11,10},{13,12},{... | collective-permute-start | bytes 20408 | tf_op jit(solution)/shard_map/ppermute | solution.py:26
  117.5 13.1 %collective-permute-start.6 = (f32[50,34,1]{0,2,1:T(1,128)S(1)}, f32[50,34,1]{0,2,1:T(1,128)S(1)}, u32[]{:S(2)}, u32[]{:S(2)}) collective-permute-start(f32[50,34,1]{0,2,1:T(1,128)S(1)} %get-tuple-element.222), channel_id=1, source_target_pairs={{0,1},{1,2},{2,3},{4,5},{5,6},{6,7},{8,9},{9,10},{10,11},{12,13},{... | collective-permute-start | bytes 20408 | tf_op jit(solution)/shard_map/ppermute | solution.py:24
  141.1 12.1 collective-permute-start.13
  193.5 10.5 collective-permute-start.19
  235.4 10.2 collective-permute-start.20
  246.5 10.2 collective-permute-start.22
  250.7 10.4 collective-permute-start.23
  263.6 16.9 %collective-permute-start.28 = (f32[2,16,1,128]{3,1,2,0:T(8,128)S(1)}, f32[2,16,1,128]{3,1,2,0:T(8,128)S(1)}, u32[]{:S(2)}, u32[]{:S(2)}) collective-permute-start(f32[2,16,1,128]{3,1,2,0:T(8,128)S(1)} %bitcast.373), channel_id=1, source_target_pairs={{0,4},{4,8},{8,12},{12,16},{16,20},{20,24},{24,28},{28,32},{32,36}... | collective-permute-start | bytes 49160 | tf_op jit(solution)/shard_map/ppermute | solution.py:24
  265.7 21.4 %collective-permute-start.43 = (f32[2,16,10,1]{3,1,2,0:T(8,128)S(1)}, f32[2,16,10,1]{3,1,2,0:T(8,128)S(1)}, u32[]{:S(2)}, u32[]{:S(2)}) collective-permute-start(f32[2,16,10,1]{3,1,2,0:T(8,128)S(1)} %get-tuple-element.323), channel_id=1, source_target_pairs={{1,0},{2,1},{3,2},{5,4},{6,5},{7,6},{9,8},{10,9},{11,10},{13,12},{... | collective-permute-start | bytes 3848 | tf_op jit(solution)/shard_map/ppermute | solution.py:26
  267.6 19.5 %collective-permute-start.42 = (f32[2,16,10,1]{3,1,2,0:T(8,128)S(1)}, f32[2,16,10,1]{3,1,2,0:T(8,128)S(1)}, u32[]{:S(2)}, u32[]{:S(2)}) collective-permute-start(f32[2,16,10,1]{3,1,2,0:T(8,128)S(1)} %get-tuple-element.322), channel_id=1, source_target_pairs={{0,1},{1,2},{2,3},{4,5},{5,6},{6,7},{8,9},{9,10},{10,11},{12,13},{... | collective-permute-start | bytes 3848 | tf_op jit(solution)/shard_map/ppermute | solution.py:24
  271.3 10.1 collective-permute-start.29
  292.6 10.1 collective-permute-start.32
  303.7 9.7 collective-permute-start.35
  327.1 11.1 collective-permute-start.37
  345.5 10.8 collective-permute-start.39
  347.5 10.3 collective-permute-start.38
  1076.6 9.8 collective-permute-start.64
  1087.4 9.9 collective-permute-start.67
  1101.2 11.2 collective-permute-start.68
  1103.2 10.1 collective-permute-start.69
  1140.0 11.0 collective-permute-start.73
  (442 other events, 4137.2 us)
where the time goes:
time: 1230 us; the launch traced here: 1210 us
  starting transfers between devices  541 us (44%)
  other arithmetic  270 us (22%)
  waiting for transfers between devices  211 us (17%)
  local copies, waits for them, and re-layouts  182 us (15%)
    ppermute x78, starting transfers between devices, padded_2(): lax.ppermute(tail, axis, [(i, (i + 1) % count) for i in range(ends)])  305 us
    ppermute x78, starting transfers between devices, padded_2(): lax.ppermute(head, axis, [((i + 1) % count, i) for i in range(ends)])  236 us
    ppermute x78, waiting for transfers between devices, padded_2(): lax.ppermute(tail, axis, [(i, (i + 1) % count) for i in range(ends)])  181 us
    another operation x96, other arithmetic, apply_operator(): return (jnp.stack(images), jnp.stack(diagonals))  79.2 us
    concatenate x73, other arithmetic, padded_2(): jnp.concatenate([lax.ppermute(tail, axis, [(i, (i + 1) % count) for i in...  51.7 us
    slice x71, local copies, waits for them, and re-layouts, padded_2(): lax.slice_in_dim(cells, cells.shape[dim] - width, cells.shape[dim], axis=...  33.1 us
    reduce_sum x6, other arithmetic, restrict(): return jnp.mean(blocks, axis=(-3, -1))  31.4 us
    ppermute x78, waiting for transfers between devices, padded_2(): lax.ppermute(head, axis, [((i + 1) % count, i) for i in range(ends)])  30 us
  transfers between devices with their start and end apart: 156, of which 94 were waited for; matrix products, arithmetic and copies ran while one was open for 12% of the time, Pallas kernels for 0%

commit v1 on v0

v1 whole, which is shorter than its diff:
```python
import functools

import jax
import jax.numpy as jnp
from jax import lax
from jax.experimental import pallas as pl
from jax.experimental.pallas import tpu as pltpu
from jax.sharding import PartitionSpec as P

MESH = pl.DeviceIdType.MESH
HBM = pltpu.MemorySpace.HBM
OMEGA = 0.6
CROSS = 0.75
ITERS = 20

OX = (32, 16, 8, 4)
OY = (256, 128, 64, 32)
LN = (384, 256, 128, 128)
RIM = (4, 5, 6, 24)
PW = (4, 8, 16, 32)
TX = tuple(o + 2 * h for o, h in zip(OX, RIM))
REACH = 6
FAR = 2 * REACH + 1
SIDES = ((0, -1), (0, 1), (-1, -1), (-1, 1), (1, -1), (1, 1))


def lane_iota(rows):
    return lax.broadcasted_iota(jnp.int32, (rows, 128), 1)


def roll(x, shift, axis):
    return pltpu.roll(x, shift % x.shape[axis], axis)


def exact_dot(x, sel):
    hi = x.astype(jnp.bfloat16)
    rest = x - hi.astype(jnp.float32)
    mid = rest.astype(jnp.bfloat16)
    low = (rest - mid.astype(jnp.float32)).astype(jnp.bfloat16)
    rows = x.shape[0]
    out = jnp.dot(
        jnp.concatenate([hi, mid, low], 0), sel, preferred_element_type=jnp.float32
    )
    return (out[:rows] + out[rows : 2 * rows]) + out[2 * rows :]


def restrict_matrix(level):
    width = min(LN[level], OY[level]) if OY[level] >= 128 else 128
    fine = lax.broadcasted_iota(jnp.int32, (width, 128), 0)
    coarse = lax.broadcasted_iota(jnp.int32, (width, 128), 1)
    hit = (fine // 2 == coarse) & (fine < OY[level])
    return jnp.where(hit, 0.25, 0.0).astype(jnp.bfloat16)


def prolong_matrix(level):
    lc, lf = LN[level + 1], LN[level]
    coarse = lax.broadcasted_iota(jnp.int32, (lc, lf), 0)
    fine = lax.broadcasted_iota(jnp.int32, (lc, lf), 1)
    middle = (OY[level] + lf) // 2
    source = jnp.where(fine < middle, fine // 2, lc - (lf - fine + 1) // 2)
    return jnp.where(source == coarse, 1.0, 0.0).astype(jnp.bfloat16)


class Message:
    def __init__(self, place, sems, index, src, dst, dx, dy):
        gx, gy, nx, ny = place
        self.to_there = (gx + dx >= 0) & (gx + dx < nx) & (gy + dy >= 0) & (gy + dy < ny)
        self.from_there = (gx - dx >= 0) & (gx - dx < nx) & (gy - dy >= 0) & (gy - dy < ny)
        target = (jnp.clip(gx + dx, 0, nx - 1), jnp.clip(gy + dy, 0, ny - 1))
        self.dst = dst
        self.copy = pltpu.make_async_remote_copy(
            src_ref=src,
            dst_ref=dst,
            send_sem=sems[0].at[index],
            recv_sem=sems[1].at[index],
            device_id=target,
            device_id_type=MESH,
        )

    def clear(self):
        @pl.when(jnp.logical_not(self.from_there))
        def _():
            self.dst[...] = jnp.zeros(self.dst.shape, self.dst.dtype)

    def start(self):
        @pl.when(self.to_there)
        def _():
            self.copy.start()

    def arrived(self):
        @pl.when(self.from_there)
        def _():
            self.copy.wait_recv()

    def sent(self):
        @pl.when(self.to_there)
        def _():
            self.copy.wait_send()


def pack_columns(level, source, dest, planes):
    w, rim = PW[level], RIM[level]
    lane = lane_iota(planes)
    tile = (OY[level] - 1) // 128
    edge = (OY[level] - w) % 128

    def body(i, acc):
        left, right = acc
        here = (lane >= w * i) & (lane < w * i + w)
        a = source[rim + i, :, 0:128]
        b = source[rim + i, :, tile * 128 : tile * 128 + 128]
        left = jnp.where(here, pltpu.roll(a, w * i, 1), left)
        right = jnp.where(here, pltpu.roll(b, lax.rem(w * i + 128 - edge, 128), 1), right)
        return left, right

    zero = jnp.zeros((planes, 128), jnp.float32)
    left, right = lax.fori_loop(0, OX[level], body, (zero, zero), unroll=4)
    dest[0] = left
    dest[1] = right


def unpack_columns(level, dest, packs, planes, reach):
    w, rim, own = PW[level], RIM[level], OX[level]
    lane = lane_iota(planes)
    last = LN[level] - 128
    start = OY[level] % 128
    for row0, count, shift, pl_left, pl_right in (
        (-reach, reach, own - reach, 2, 3),
        (0, own, 0, 0, 1),
        (own, reach, 0, 4, 5),
    ):

        def body(i, _, row0=row0, shift=shift, pl_left=pl_left, pl_right=pl_right):
            at = w * (i + shift)
            right = pltpu.roll(packs[pl_right], lax.rem(start - at + 128, 128), 1)
            left = pltpu.roll(packs[pl_left], lax.rem(256 - w - at, 128), 1)
            row = rim + row0 + i
            if OY[level] < 128:
                base = dest[row, :, last : last + 128]
            else:
                base = jnp.zeros((planes, 128), jnp.float32)
            tile = jnp.where((lane >= start) & (lane < start + w), right, base)
            dest[row, :, last : last + 128] = jnp.where(lane >= 128 - w, left, tile)
            return 0

        lax.fori_loop(0, count, body, 0, unroll=2 if count % 2 == 0 else 1)


def coefficients(level, c, e, y4, z, q, r, g, rows):
    scale = 0.25**level
    half, cross = 0.5 * scale, CROSS * scale
    lanes, rim = LN[level], RIM[level]
    first, count = rim - rows, OX[level] + 2 * rows
    sub = lax.broadcasted_iota(jnp.int32, (8, lanes), 0)
    e[first - 1] = half * (c[first - 1, 0:16, :] + c[first, 0:16, :])

    def body(n, _):
        i = first + n
        here = c[i, 0:16, :]
        north, south = roll(here, -1, 1), roll(here, 1, 1)
        east = half * (here + c[i + 1, 0:16, :])
        west = half * (here + c[i - 1, 0:16, :])
        nf, sf = half * (here + north), half * (here + south)
        e[i] = east
        y4[i, 0:16, :] = nf
        y4[i, 16:32, :] = sf
        y4[i, 32:48, :] = cross * north
        y4[i, 48:64, :] = cross * south
        even, odd = here[0:8], here[8:16]
        inner = 2.0 * (even + odd)
        upper = jnp.where(sub < 7, 2.0 * (odd + roll(even, -1, 0)), 0.0)
        lower = roll(upper, 1, 0)
        z[i, 0:8, :] = inner
        z[i, 8:16, :] = upper
        z[i, 16:24, :] = lower
        ice = c[i, 16:17, :]
        drag = jnp.where(sub == 0, c[i, 17:18, :], 0.0)
        vertical = jnp.concatenate([inner + lower + drag, inner + upper], 0)
        xs, ys = east + west, nf + sf
        for k, lateral in enumerate((4.0 * xs + ys, xs + 4.0 * ys)):
            diag = ice * (lateral + vertical) + (1.0 - ice)
            inv = OMEGA / diag
            if q is not None:
                q[i, 16 * k : 16 * k + 16, :] = inv
            r[i, 16 * k : 16 * k + 16, :] = ice * inv
            if g is not None:
                g[i, 16 * k : 16 * k + 16, :] = diag * (1.0 / OMEGA)
        return 0

    lax.fori_loop(0, count, body, 0)


def off_diagonal(w, e, y4, z, i):
    u0, u, u2 = w[i - 1, 0:16, :], w[i, 0:16, :], w[i + 1, 0:16, :]
    v0, v, v2 = w[i - 1, 16:32, :], w[i, 16:32, :], w[i + 1, 16:32, :]
    west, east = e[i - 1], e[i]
    nf, sf, mn, ms = (y4[i, 16 * k : 16 * k + 16, :] for k in range(4))
    inner, upper, lower = (z[i, 8 * k : 8 * k + 8, :] for k in range(3))
    du, dv, v4 = u2 - u0, v2 - v0, 4.0 * v
    xu = 4.0 * (east * u2 + west * u0)
    xv = east * v2 + west * v0
    yu = roll(sf * u + ms * dv, -1, 1) + roll(nf * u - mn * dv, 1, 1)
    yv = roll(sf * v4 + ms * du, -1, 1) + roll(nf * v4 - mn * du, 1, 1)

    def column(f):
        even, odd = f[0:8], f[8:16]
        return jnp.concatenate(
            [inner * odd + lower * roll(odd, 1, 0), inner * even + upper * roll(even, -1, 0)], 0
        )

    return (u, v), (xu + yu + column(u), xv + yv + column(v))


def sweep_row(src, dst, e, y4, z, r, tt, i):
    fields, sums = off_diagonal(src, e, y4, z, i)
    for k in range(2):
        at = slice(16 * k, 16 * k + 16)
        dst[i, at, :] = (1.0 - OMEGA) * fields[k] + (tt[i, at, :] + r[i, at, :] * sums[k])


def remainder_row(src, e, y4, z, r, tt, g, i, lanes):
    fields, sums = off_diagonal(src, e, y4, z, i)
    parts = []
    for k in range(2):
        at = slice(16 * k, 16 * k + 16)
        change = tt[i, at, :] + r[i, at, :] * sums[k] - OMEGA * fields[k]
        parts.append(change[:, 0:lanes] * g[i, at, 0:lanes])
    return jnp.concatenate(parts, 0)


def kernel(nx, ny, m_ref, v_ref, f_ref, i_ref, b_ref, o_ref, *scratch):
    names = iter(scratch)
    lv = []
    for level in range(4):
        keys = ["c", "e", "y4", "z", "r", "t", "a", "b"]
        keys += ["q"] if level > 0 else []
        keys += ["g"] if level < 3 else []
        keys += ["spc", "rpc", "spt", "rpt"] if level < 3 else []
        lv.append({key: next(names) for key in keys})
    rest, far_c, far_t, side_c, side_t, fr, ic, gr = (next(names) for _ in range(8))
    in_sem, out_sem, send_sem, recv_sem, l3c, l3t = (next(names) for _ in range(6))

    gx, gy = lax.axis_index("gx"), lax.axis_index("gy")
    place = (gx, gy, nx, ny)
    sems = (send_sem, recv_sem)
    count = iter(range(10**6))

    def message(src, dst, dx, dy):
        return Message(place, sems, next(count), src, dst, dx, dy)

    def rim_messages(level, array, packs, landed, reach):
        rim, own = RIM[level], OX[level]
        lanes = pl.ds(0, max(OY[level], 128))
        out = [
            message(
                array.at[pl.ds(rim, reach), :, lanes],
                array.at[pl.ds(rim + own, reach), :, lanes], -1, 0),
            message(
                array.at[pl.ds(rim + own - reach, reach), :, lanes],
                array.at[pl.ds(rim - reach, reach), :, lanes], 1, 0),
        ]
        for slot, (dx, dy) in enumerate(SIDES):
            out.append(message(packs.at[0 if dy > 0 else 1], landed.at[slot], -dx, -dy))
        return out

    def far_messages(own, far):
        return [
            message(far.at[REACH], far.at[REACH - d], d, 0)
            for d in [k * s for k in range(REACH, 0, -1) for s in (1, -1)]
        ]

    def side_messages(far, side):
        return [message(far, side.at[0], 0, 1), message(far, side.at[1], 0, -1)]

    msg_c = [rim_messages(n, lv[n]["c"], lv[n]["spc"], lv[n]["rpc"], RIM[n]) for n in range(3)]
    msg_t = [rim_messages(n, lv[n]["t"], lv[n]["spt"], lv[n]["rpt"], RIM[n] - 1) for n in range(3)]
    msg_fc, msg_ft = far_messages(None, far_c), far_messages(None, far_t)
    msg_sc, msg_st = side_messages(far_c, side_c), side_messages(far_t, side_t)
    every = sum(msg_c + msg_t, []) + msg_fc + msg_ft + msg_sc + msg_st

    own0 = pl.ds(RIM[0], OX[0])
    loads = []
    for k in range(16):
        kk = (k % 2) * 8 + k // 2
        loads.append((v_ref.at[k], lv[0]["c"].at[own0, kk, pl.ds(0, 256)]))
        for n in range(2):
            loads.append((m_ref.at[n, k], lv[0]["t"].at[own0, 16 * n + kk, pl.ds(0, 256)]))
    loads += [(f_ref, fr), (i_ref, ic), (b_ref, gr)]
    loads = [pltpu.make_async_copy(s, d, in_sem.at[n]) for n, (s, d) in enumerate(loads)]
    for load in loads:
        load.start()

    barrier = pltpu.get_barrier_semaphore()
    partners = [(d, 0) for d in range(-REACH, REACH + 1) if d != 0] + list(SIDES)
    arrivals = 0
    for dx, dy in partners:
        there = (gx + dx >= 0) & (gx + dx < nx) & (gy + dy >= 0) & (gy + dy < ny)
        arrivals = arrivals + there.astype(jnp.int32)

        @pl.when(there)
        def _(dx=dx, dy=dy):
            pl.semaphore_signal(
                barrier,
                inc=1,
                device_id=(jnp.clip(gx + dx, 0, nx - 1), jnp.clip(gy + dy, 0, ny - 1)),
                device_id_type=MESH,
            )

    for one in every:
        one.clear()
    for load in loads:
        load.wait()

    c0, t0 = lv[0]["c"], lv[0]["t"]
    ic_f = ic[...].astype(jnp.float32)
    ic_f = ic_f.reshape(OX[0], 1, 256)
    dr_f = (fr[...] * gr[...].astype(jnp.float32)).reshape(OX[0], 1, 256)
    sub = lax.broadcasted_iota(jnp.int32, (OX[0], 8, 256), 1)
    c0[own0, 16:24, 0:256] = jnp.where(sub == 0, ic_f, jnp.where(sub == 1, dr_f, 0.0))

    pl.semaphore_wait(barrier, arrivals)
    for one in msg_c[0][:2] + msg_t[0][:2]:
        one.start()
    pack_columns(0, c0, lv[0]["spc"], 24)
    pack_columns(0, t0, lv[0]["spt"], 32)
    for one in msg_c[0][2:] + msg_t[0][2:]:
        one.start()

    for level in range(3):
        rim, own, width = RIM[level], OX[level + 1], max(OY[level], 128)
        fine = lv[level]["c"]
        block = fine[rim : rim + 2 * own, :, 0:width].reshape(own, 2, 24, width)
        block = (block[:, 0] + block[:, 1]).reshape(own * 24, width)
        coarse = exact_dot(block, restrict_matrix(level)).reshape(own, 24, 128)
        if level < 2:
            target = lv[level + 1]["c"]
            target[RIM[level + 1] : RIM[level + 1] + own, :, 0:128] = coarse
            for one in msg_c[level + 1][:2]:
                one.start()
            pack_columns(level + 1, target, lv[level + 1]["spc"], 24)
            for one in msg_c[level + 1][2:]:
                one.start()
        else:
            far_c[REACH] = sum(roll(coarse[k], 32 * k, 1) for k in range(4))
            for one in msg_fc:
                one.start()

    def refs(level):
        return [lv[level][key] for key in ("e", "y4", "z", "r", "t")]

    def gather(level, kind, messages, landed, planes, reach):
        for one in messages:
            one.arrived()
        if OY[level] < 128:
            for one in messages[:2]:
                one.sent()
        unpack_columns(level, lv[level][kind], lv[level][landed], planes, reach)

    def first_sweep(level, rows, factor):
        t = lv[level]["t"]

        def body(n, _):
            i = RIM[level] - rows + n
            t[i] = t[i] * factor[i]
            return 0

        lax.fori_loop(0, OX[level] + 2 * rows, body, 0, unroll=2)

    def sweep(level, src, dst, rows):
        args = refs(level)

        def body(n, _):
            sweep_row(src, dst, *args, RIM[level] - rows + n)
            return 0

        lax.fori_loop(0, OX[level] + 2 * rows, body, 0, unroll=1 if level < 2 else 2)

    def restricted_remainder(level, src):
        args = refs(level)
        width, own = max(OY[level], 128), OX[level + 1]

        def body(n, _):
            i = RIM[level] + 2 * n
            pair = [remainder_row(src, *args, lv[level]["g"], i + k, width) for k in range(2)]
            rest[n, :, 0:width] = pair[0] + pair[1]
            return 0

        lax.fori_loop(0, own, body, 0)
        block = rest[0:own, :, 0:width].reshape(own * 32, width)
        return exact_dot(block, restrict_matrix(level)).reshape(own, 32, 128)

    def prolonged(level, src, dst, rows):
        low, high = RIM[level + 1] - rows, RIM[level + 1] + OX[level + 1] + rows
        n = high - low
        sel = prolong_matrix(level)
        spread = lv[level]["g"]
        block = src[low:high].reshape(n * 32, LN[level + 1])
        spread[0:n] = exact_dot(block, sel).reshape(n, 32, LN[level])

        def body(k, _):
            i = RIM[level] + 2 * (k - rows)
            extra = spread[k]
            dst[i] = dst[i] + extra
            dst[i + 1] = dst[i + 1] + extra
            return 0

        lax.fori_loop(0, n, body, 0)

    gather(0, "c", msg_c[0], "rpc", 24, RIM[0])
    coefficients(0, c0, *[lv[0][k] for k in ("e", "y4", "z")], None, lv[0]["r"], lv[0]["g"], 3)
    gather(0, "t", msg_t[0], "rpt", 32, RIM[0] - 1)
    for one in msg_t[0][:2]:
        one.sent()
    first_sweep(0, 3, lv[0]["r"])
    sweep(0, t0, lv[0]["a"], 2)
    t_next = restricted_remainder(0, lv[0]["a"])

    for level in (1, 2):
        t = lv[level]["t"]
        t[RIM[level] : RIM[level] + OX[level], :, 0:128] = t_next
        for one in msg_t[level][:2]:
            one.start()
        pack_columns(level, t, lv[level]["spt"], 32)
        for one in msg_t[level][2:]:
            one.start()
        gather(level, "c", msg_c[level], "rpc", 24, RIM[level])
        coefficients(
            level, *[lv[level][k] for k in ("c", "e", "y4", "z", "q", "r", "g")], RIM[level] - 1
        )
        if level == 1:
            for one in msg_fc:
                one.arrived()
            for one in msg_sc:
                one.start()
        gather(level, "t", msg_t[level], "rpt", 32, RIM[level] - 1)
        if OY[level] >= 128:
            for one in msg_t[level][:2]:
                one.sent()
        first_sweep(level, RIM[level] - 1, lv[level]["q"])
        sweep(level, t, lv[level]["a"], RIM[level] - 2)
        t_next = restricted_remainder(level, lv[level]["a"])

    far_t[REACH] = sum(roll(t_next[k], 32 * k, 1) for k in range(4))
    for one in msg_ft:
        one.start()

    def unpack_far(dest, far, side, planes):
        lane = lane_iota(planes)

        def body(b, _):
            own, left, right = far[b], side[0, b], side[1, b]
            for k in range(4):
                tile = jnp.where(lane < 32, roll(own, -32 * k, 1), 0.0)
                tile = jnp.where((lane >= 32) & (lane < 64), roll(right, 32 - 32 * k, 1), tile)
                tile = jnp.where(lane >= 96, roll(left, 96 - 32 * k, 1), tile)
                dest[4 * b + k] = tile
            return 0

        lax.fori_loop(0, FAR, body, 0)

    for one in msg_sc:
        one.arrived()
    unpack_far(lv[3]["c"], far_c, side_c, 24)
    coefficients(3, *[lv[3][k] for k in ("c", "e", "y4", "z", "q", "r")], None, RIM[3] - 1)
    for one in msg_ft:
        one.arrived()
    for one in msg_st:
        one.start()
    for one in msg_st:
        one.arrived()
    t3, a3, b3 = lv[3]["t"], lv[3]["a"], lv[3]["b"]
    unpack_far(t3, far_t, side_t, 32)
    first_sweep(3, RIM[3] - 1, lv[3]["q"])
    args3 = refs(3)

    def coarse_sweep(src, dst, s):
        first = s + 2

        def body(n, _):
            for k in range(4):
                sweep_row(src, dst, *args3, first + 4 * n + k)
            return 0

        lax.fori_loop(0, (51 - 2 * s) // 4, body, 0)

    coarse_sweep(t3, a3, 2)

    def coarse_pair(n, _):
        coarse_sweep(a3, b3, 2 * n + 3)
        coarse_sweep(b3, a3, 2 * n + 4)
        return 0

    lax.fori_loop(0, (ITERS - 2) // 2, coarse_pair, 0)

    prolonged(2, a3, lv[2]["a"], 2)
    sweep(2, lv[2]["a"], lv[2]["b"], 3)
    sweep(2, lv[2]["b"], lv[2]["a"], 2)
    prolonged(1, lv[2]["a"], lv[1]["a"], 2)
    sweep(1, lv[1]["a"], lv[1]["b"], 2)
    sweep(1, lv[1]["b"], lv[1]["a"], 1)
    prolonged(0, lv[1]["a"], lv[0]["a"], 1)
    a0, b0 = lv[0]["a"], lv[0]["b"]
    sweep(0, a0, b0, 1)
    args0 = refs(0)
    stores = []
    for part in range(2):
        first = RIM[0] + 16 * part

        def last_body(n, _, first=first):
            sweep_row(b0, a0, *args0, first + n)
            return 0

        lax.fori_loop(0, 16, last_body, 0)
        for n in range(2):
            for k in range(16):
                kk = (k % 2) * 8 + k // 2
                store = pltpu.make_async_copy(
                    a0.at[pl.ds(first, 16), 16 * n + kk, pl.ds(0, 256)],
                    o_ref.at[n, k, pl.ds(16 * part, 16), :],
                    out_sem.at[32 * part + 16 * n + k],
                )
                store.start()
                stores.append(store)
    waited = msg_t[0][:2] + msg_t[1][:2] + msg_t[2][:2] + msg_c[2][:2]
    for one in every:
        if one not in waited:
            one.sent()
    for store in stores:
        store.wait()


def solution(mesh):
    nx, ny = mesh.shape["gx"], mesh.shape["gy"]
    f32 = jnp.float32
    scratch = []
    for level in range(4):
        rows, lanes = TX[level], LN[level]
        planes = [24, 16, 64, 24, 32, 32, 32, 32]
        planes += [32] if level > 0 else []
        planes += [32] if level < 3 else []
        scratch += [pltpu.VMEM((rows, p, lanes), f32) for p in planes]
        if level < 3:
            scratch += [pltpu.VMEM((n, p, 128), f32) for p in (24, 32) for n in (2, 6)]
    scratch += [pltpu.VMEM((16, 32, 256), f32)]
    scratch += [pltpu.VMEM((FAR, 24, 128), f32), pltpu.VMEM((FAR, 32, 128), f32)]
    scratch += [pltpu.VMEM((2, FAR, 24, 128), f32), pltpu.VMEM((2, FAR, 32, 128), f32)]
    scratch += [
        pltpu.VMEM((32, 256), f32),
        pltpu.VMEM((32, 256), jnp.int32),
        pltpu.VMEM((32, 256), jnp.int32),
    ]
    messages = 6 * 8 + 4 * REACH + 4
    scratch += [pltpu.SemaphoreType.DMA((51,)), pltpu.SemaphoreType.DMA((64,))]
    scratch += [pltpu.SemaphoreType.DMA((messages,)), pltpu.SemaphoreType.DMA((messages,))]
    scratch += [pltpu.SemaphoreType.DMA((1,)), pltpu.SemaphoreType.DMA((1,))]

    def per_device(misfit, viscosity, friction, ice_mask, grounded):
        return pl.pallas_call(
            functools.partial(kernel, nx, ny),
            out_shape=jax.ShapeDtypeStruct(misfit.shape, f32),
            in_specs=[pl.BlockSpec(memory_space=HBM)] * 5,
            out_specs=pl.BlockSpec(memory_space=HBM),
            scratch_shapes=scratch,
            compiler_params=pltpu.CompilerParams(
                collective_id=0, has_side_effects=True, vmem_limit_bytes=62 * 2**20
            ),
        )(misfit, viscosity, friction, ice_mask, grounded)

    placed = (
        P(None, None, "gx", "gy"),
        P(None, "gx", "gy"),
        P("gx", "gy"),
        P("gx", "gy"),
        P("gx", "gy"),
    )
    return jax.shard_map(
        per_device, mesh=mesh, in_specs=placed, out_specs=P(None, None, "gx", "gy"), check_vma=False
    )
```

time: 1230 us -> 99.1 us (0.08); the launches traced: 1210 us -> 98 us
  starting transfers between devices: 541 us -> 0 us
  other arithmetic: 270 us -> 0 us
  waiting for transfers between devices: 211 us -> 0 us
  local copies, waits for them, and re-layouts: 182 us -> 2.31 us
  Pallas kernels: 0 us -> 95.6 us
    ppermute x156 -> x0, starting transfers between devices: 541 us -> none  [the longest x78 305 us: padded_2(): lax.ppermute(tail, axis, [(i, (i + 1) % count) for i in range(ends)])]
    ppermute x156 -> x0, waiting for transfers between devices: 211 us -> none  [the longest x78 181 us: padded_2(): lax.ppermute(tail, axis, [(i, (i + 1) % count) for i in range(ends)])]
    pallas_call x0 -> x1, Pallas kernels: none -> 95.6 us  [per_device(): pl.pallas_call(functools.partial(kernel, nx, ny), out_shape=jax.ShapeDtyp...]
    another operation x96 -> x0, other arithmetic: 79.2 us -> none  [apply_operator(): return (jnp.stack(images), jnp.stack(diagonals))]
    mul x62 -> x0, other arithmetic: 54.6 us -> none  [the longest x22 27.2 us: apply_operator(): images.append(ice_share * flow + (1.0 - ice_share) * middle)]
    concatenate x76 -> x0, other arithmetic: 51.9 us -> none  [the longest x73 51.7 us: padded_2(): jnp.concatenate([lax.ppermute(tail, axis, [(i, (i + 1) % count) for i in...]
    slice x93 -> x0, local copies, waits for them, and re-layouts: 44 us -> none  [the longest x71 33.1 us: padded_2(): lax.slice_in_dim(cells, cells.shape[dim] - width, cells.shape[dim], axis=...]
    reduce_sum x6 -> x0, other arithmetic: 31.4 us -> none  [restrict(): return jnp.mean(blocks, axis=(-3, -1))]
  transfers between devices with their start and end apart: 156 -> 0, of which waited for: 94 -> 0; matrix products, arithmetic and copies ran while one was open for 12% -> 0% of each run, Pallas kernels for 0% -> 0%
where the time goes in v1:
time: 99.1 us; the launch traced here: 98 us
  Pallas kernels  95.6 us (96%)
  local copies, waits for them, and re-layouts  2.31 us (2%)
    pallas_call x1, Pallas kernels, per_device(): pl.pallas_call(functools.partial(kernel, nx, ny), out_shape=jax.ShapeDtyp...  95.6 us
    unnamed x1, local copies, waits for them, and re-layouts  2.31 us

profile of v1, /device:TPU:5, one launch (start us, length us, event | category | flops | bytes accessed | tf_op | source)
XLA Modules:
  0.0 98.0 jit_solution(4979945910411985781)
XLA Ops:
  0.0 95.6 %shard_map.55 = f32[2,16,32,256]{3,2,1,0:T(8,128)} custom-call(f32[2,16,32,256]{3,2,1,0:T(8,128)} %m_ref.1, f32[16,32,256]{2,1,0:T(8,128)} %v_ref.1, f32[32,256]{1,0:T(8,128)} %f_ref.1, s32[32,256]{1,0:T(8,128)} %i_ref.1, s32[32,256]{1,0:T(8,128)} %b_ref.1), custom_call_target="tpu_custom_call" | custom-call | tf_op jit(solution)/shard_map/pallas_call | solution.py:558
  95.6 2.3 %copy.7 = f32[2,16,32,256]{3,2,1,0:T(8,128)} copy(f32[2,16,32,256]{3,2,1,0:T(8,128)} %shard_map.55) | data formatting | bytes 2097152

commit v2 on v1

--- a/solution.py
+++ b/solution.py
@@ -18,10 +18,27 @@
 LN = (384, 256, 128, 128)
 RIM = (4, 5, 6, 24)
 PW = (4, 8, 16, 32)
-TX = tuple(o + 2 * h for o, h in zip(OX, RIM))
+TX = tuple(o + 2 * h for o, h in zip(OX[:3], RIM)) + (58,)
+UNROLL = (2, 3, 6, 8)
+UNROLL_C = (2, 3, 6, 5)
+UNROLL_R = (1, 2, 4)
 REACH = 6
 FAR = 2 * REACH + 1
 SIDES = ((0, -1), (0, 1), (-1, -1), (-1, 1), (1, -1), (1, 1))
+
+
+def over_rows(first, count, body, unroll):
+    steps = count // unroll
+
+    def step(n, _):
+        for k in range(unroll):
+            body(first + n * unroll + k)
+        return 0
+
+    if steps > 0:
+        lax.fori_loop(0, steps, step, 0)
+    for k in range(steps * unroll, count):
+        body(first + k)
 
 
 def lane_iota(rows):
@@ -130,10 +147,10 @@
         (own, reach, 0, 4, 5),
     ):
 
-        def body(i, _, row0=row0, shift=shift, pl_left=pl_left, pl_right=pl_right):
+        for i in range(count):
             at = w * (i + shift)
-            right = pltpu.roll(packs[pl_right], lax.rem(start - at + 128, 128), 1)
-            left = pltpu.roll(packs[pl_left], lax.rem(256 - w - at, 128), 1)
+            right = roll(packs[pl_right], start - at, 1)
+            left = roll(packs[pl_left], -w - at, 1)
             row = rim + row0 + i
             if OY[level] < 128:
                 base = dest[row, :, last : last + 128]
@@ -141,9 +158,6 @@
                 base = jnp.zeros((planes, 128), jnp.float32)
             tile = jnp.where((lane >= start) & (lane < start + w), right, base)
             dest[row, :, last : last + 128] = jnp.where(lane >= 128 - w, left, tile)
-            return 0
-
-        lax.fori_loop(0, count, body, 0, unroll=2 if count % 2 == 0 else 1)
 
 
 def coefficients(level, c, e, y4, z, q, r, g, rows):
@@ -154,8 +168,7 @@
     sub = lax.broadcasted_iota(jnp.int32, (8, lanes), 0)
     e[first - 1] = half * (c[first - 1, 0:16, :] + c[first, 0:16, :])
 
-    def body(n, _):
-        i = first + n
+    def body(i):
         here = c[i, 0:16, :]
         north, south = roll(here, -1, 1), roll(here, 1, 1)
         east = half * (here + c[i + 1, 0:16, :])
@@ -185,9 +198,8 @@
             r[i, 16 * k : 16 * k + 16, :] = ice * inv
             if g is not None:
                 g[i, 16 * k : 16 * k + 16, :] = diag * (1.0 / OMEGA)
-        return 0
-
-    lax.fori_loop(0, count, body, 0)
+
+    over_rows(first, count, body, UNROLL_C[level])
 
 
 def off_diagonal(w, e, y4, z, i):
@@ -238,7 +250,7 @@
         keys += ["spc", "rpc", "spt", "rpt"] if level < 3 else []
         lv.append({key: next(names) for key in keys})
     rest, far_c, far_t, side_c, side_t, fr, ic, gr = (next(names) for _ in range(8))
-    in_sem, out_sem, send_sem, recv_sem, l3c, l3t = (next(names) for _ in range(6))
+    in_sem, out_sem, send_sem, recv_sem = (next(names) for _ in range(4))
 
     gx, gy = lax.axis_index("gx"), lax.axis_index("gy")
     place = (gx, gy, nx, ny)
@@ -359,33 +371,31 @@
     def first_sweep(level, rows, factor):
         t = lv[level]["t"]
 
-        def body(n, _):
-            i = RIM[level] - rows + n
+        def body(i):
             t[i] = t[i] * factor[i]
-            return 0
-
-        lax.fori_loop(0, OX[level] + 2 * rows, body, 0, unroll=2)
+
+        over_rows(RIM[level] - rows, OX[level] + 2 * rows, body, 4)
 
     def sweep(level, src, dst, rows):
         args = refs(level)
 
-        def body(n, _):
-            sweep_row(src, dst, *args, RIM[level] - rows + n)
-            return 0
-
-        lax.fori_loop(0, OX[level] + 2 * rows, body, 0, unroll=1 if level < 2 else 2)
+        over_rows(
+            RIM[level] - rows,
+            OX[level] + 2 * rows,
+            lambda i: sweep_row(src, dst, *args, i),
+            UNROLL[level],
+        )
 
     def restricted_remainder(level, src):
         args = refs(level)
         width, own = max(OY[level], 128), OX[level + 1]
 
-        def body(n, _):
+        def body(n):
             i = RIM[level] + 2 * n
             pair = [remainder_row(src, *args, lv[level]["g"], i + k, width) for k in range(2)]
             rest[n, :, 0:width] = pair[0] + pair[1]
-            return 0
-
-        lax.fori_loop(0, own, body, 0)
+
+        over_rows(0, own, body, UNROLL_R[level])
         block = rest[0:own, :, 0:width].reshape(own * 32, width)
         return exact_dot(block, restrict_matrix(level)).reshape(own, 32, 128)
 
@@ -397,14 +407,13 @@
         block = src[low:high].reshape(n * 32, LN[level + 1])
         spread[0:n] = exact_dot(block, sel).reshape(n, 32, LN[level])
 
-        def body(k, _):
+        def body(k):
             i = RIM[level] + 2 * (k - rows)
             extra = spread[k]
             dst[i] = dst[i] + extra
             dst[i + 1] = dst[i + 1] + extra
-            return 0
-
-        lax.fori_loop(0, n, body, 0)
+
+        over_rows(0, n, body, 2)
 
     gather(0, "c", msg_c[0], "rpc", 24, RIM[0])
     coefficients(0, c0, *[lv[0][k] for k in ("e", "y4", "z")], None, lv[0]["r"], lv[0]["g"], 3)
@@ -477,11 +486,11 @@
         first = s + 2
 
         def body(n, _):
-            for k in range(4):
-                sweep_row(src, dst, *args3, first + 4 * n + k)
+            for k in range(UNROLL[3]):
+                sweep_row(src, dst, *args3, first + UNROLL[3] * n + k)
             return 0
 
-        lax.fori_loop(0, (51 - 2 * s) // 4, body, 0)
+        lax.fori_loop(0, (47 - 2 * s + UNROLL[3]) // UNROLL[3], body, 0)
 
     coarse_sweep(t3, a3, 2)
 
@@ -506,11 +515,7 @@
     for part in range(2):
         first = RIM[0] + 16 * part
 
-        def last_body(n, _, first=first):
-            sweep_row(b0, a0, *args0, first + n)
-            return 0
-
-        lax.fori_loop(0, 16, last_body, 0)
+        over_rows(first, 16, lambda i: sweep_row(b0, a0, *args0, i), UNROLL[0])
         for n in range(2):
             for k in range(16):
                 kk = (k % 2) * 8 + k // 2
@@ -552,7 +557,6 @@
     messages = 6 * 8 + 4 * REACH + 4
     scratch += [pltpu.SemaphoreType.DMA((51,)), pltpu.SemaphoreType.DMA((64,))]
     scratch += [pltpu.SemaphoreType.DMA((messages,)), pltpu.SemaphoreType.DMA((messages,))]
-    scratch += [pltpu.SemaphoreType.DMA((1,)), pltpu.SemaphoreType.DMA((1,))]
 
     def per_device(misfit, viscosity, friction, ice_mask, grounded):
         return pl.pallas_call(

time: 99.1 us -> 80.4 us (0.81)
  Pallas kernels: 95.6 us -> 77.6 us
    pallas_call x1, Pallas kernels: 95.6 us -> 77.6 us  [per_device(): pl.pallas_call(functools.partial(kernel, nx, ny), out_shape=jax.ShapeDtyp...]
where the time goes in v2:
time: 80.4 us; the launch traced here: 79.9 us
  Pallas kernels  77.6 us (97%)
  local copies, waits for them, and re-layouts  2.31 us (3%)
    pallas_call x1, Pallas kernels, per_device(): pl.pallas_call(functools.partial(kernel, nx, ny), out_shape=jax.ShapeDtyp...  77.6 us
    unnamed x1, local copies, waits for them, and re-layouts  2.31 us

profile of v2, /device:TPU:5, one launch (start us, length us, event | category | flops | bytes accessed | tf_op | source)
XLA Modules:
  0.0 79.9 jit_solution(15872920490909842042)
XLA Ops:
  0.0 77.6 %shard_map.55 = f32[2,16,32,256]{3,2,1,0:T(8,128)} custom-call(f32[2,16,32,256]{3,2,1,0:T(8,128)} %m_ref.1, f32[16,32,256]{2,1,0:T(8,128)} %v_ref.1, f32[32,256]{1,0:T(8,128)} %f_ref.1, s32[32,256]{1,0:T(8,128)} %i_ref.1, s32[32,256]{1,0:T(8,128)} %b_ref.1), custom_call_target="tpu_custom_call" | custom-call | tf_op jit(solution)/shard_map/pallas_call | solution.py:562
  77.6 2.3 %copy.7 = f32[2,16,32,256]{3,2,1,0:T(8,128)} copy(f32[2,16,32,256]{3,2,1,0:T(8,128)} %shard_map.55) | data formatting | bytes 2097152

commit v3 on v2

--- a/solution.py
+++ b/solution.py
@@ -115,56 +115,51 @@
             self.copy.wait_send()
 
 
-def pack_columns(level, source, dest, planes):
+def pack_columns(level, source, dest, planes, rows, base, start=None):
     w, rim = PW[level], RIM[level]
     lane = lane_iota(planes)
     tile = (OY[level] - 1) // 128
     edge = (OY[level] - w) % 128
-
-    def body(i, acc):
-        left, right = acc
+    zero = jnp.zeros((planes, 128), jnp.float32)
+    left, right = (zero, zero) if start is None else (dest[start], dest[start + 1])
+    for i in rows:
         here = (lane >= w * i) & (lane < w * i + w)
         a = source[rim + i, :, 0:128]
         b = source[rim + i, :, tile * 128 : tile * 128 + 128]
-        left = jnp.where(here, pltpu.roll(a, w * i, 1), left)
-        right = jnp.where(here, pltpu.roll(b, lax.rem(w * i + 128 - edge, 128), 1), right)
-        return left, right
-
-    zero = jnp.zeros((planes, 128), jnp.float32)
-    left, right = lax.fori_loop(0, OX[level], body, (zero, zero), unroll=4)
-    dest[0] = left
-    dest[1] = right
-
-
-def unpack_columns(level, dest, packs, planes, reach):
+        left = jnp.where(here, roll(a, w * i, 1), left)
+        right = jnp.where(here, roll(b, w * i - edge, 1), right)
+    dest[base] = left
+    dest[base + 1] = right
+
+
+def unpack_columns(level, dest, packs, planes, reach, side):
     w, rim, own = PW[level], RIM[level], OX[level]
     lane = lane_iota(planes)
     last = LN[level] - 128
     start = OY[level] % 128
-    for row0, count, shift, pl_left, pl_right in (
-        (-reach, reach, own - reach, 2, 3),
-        (0, own, 0, 0, 1),
-        (own, reach, 0, 4, 5),
-    ):
-
-        for i in range(count):
-            at = w * (i + shift)
-            right = roll(packs[pl_right], start - at, 1)
-            left = roll(packs[pl_left], -w - at, 1)
-            row = rim + row0 + i
-            if OY[level] < 128:
-                base = dest[row, :, last : last + 128]
-            else:
-                base = jnp.zeros((planes, 128), jnp.float32)
-            tile = jnp.where((lane >= start) & (lane < start + w), right, base)
-            dest[row, :, last : last + 128] = jnp.where(lane >= 128 - w, left, tile)
-
-
-def coefficients(level, c, e, y4, z, q, r, g, rows):
+    row0, count, shift, slot = {
+        -1: (-reach, reach, own - reach, 2),
+        0: (0, own, 0, 0),
+        1: (own, reach, 0, 4),
+    }[side]
+    for i in range(count):
+        at = w * (i + shift)
+        right = roll(packs[slot + 1], start - at, 1)
+        left = roll(packs[slot], -w - at, 1)
+        row = rim + row0 + i
+        if OY[level] < 128:
+            rest = dest[row, :, last : last + 128]
+        else:
+            rest = jnp.zeros((planes, 128), jnp.float32)
+        tile = jnp.where((lane >= start) & (lane < start + w), right, rest)
+        dest[row, :, last : last + 128] = jnp.where(lane >= 128 - w, left, tile)
+
+
+def coefficients(level, c, e, y4, z, q, r, g, low, high):
     scale = 0.25**level
     half, cross = 0.5 * scale, CROSS * scale
     lanes, rim = LN[level], RIM[level]
-    first, count = rim - rows, OX[level] + 2 * rows
+    first, count = rim + low, high - low
     sub = lax.broadcasted_iota(jnp.int32, (8, lanes), 0)
     e[first - 1] = half * (c[first - 1, 0:16, :] + c[first, 0:16, :])
 
@@ -248,6 +243,7 @@
         keys += ["q"] if level > 0 else []
         keys += ["g"] if level < 3 else []
         keys += ["spc", "rpc", "spt", "rpt"] if level < 3 else []
+        keys += ["raw"] if level == 0 else []
         lv.append({key: next(names) for key in keys})
     rest, far_c, far_t, side_c, side_t, fr, ic, gr = (next(names) for _ in range(8))
     in_sem, out_sem, send_sem, recv_sem = (next(names) for _ in range(4))
@@ -260,7 +256,7 @@
     def message(src, dst, dx, dy):
         return Message(place, sems, next(count), src, dst, dx, dy)
 
-    def rim_messages(level, array, packs, landed, reach):
+    def rim_messages(level, array, packs, landed, reach, corner):
         rim, own = RIM[level], OX[level]
         lanes = pl.ds(0, max(OY[level], 128))
         out = [
@@ -272,23 +268,31 @@
                 array.at[pl.ds(rim - reach, reach), :, lanes], 1, 0),
         ]
         for slot, (dx, dy) in enumerate(SIDES):
-            out.append(message(packs.at[0 if dy > 0 else 1], landed.at[slot], -dx, -dy))
+            pack = (0 if dy > 0 else 1) + (corner if dx != 0 else 0)
+            out.append(message(packs.at[pack], landed.at[slot], -dx, -dy))
         return out
 
-    def far_messages(own, far):
+    def far_messages(far):
+        order = [k * s for k in range(REACH, 0, -1) for s in (1, -1)]
+        return {d: message(far.at[REACH], far.at[REACH - d], d, 0) for d in order}
+
+    def side_messages(far, side):
         return [
-            message(far.at[REACH], far.at[REACH - d], d, 0)
-            for d in [k * s for k in range(REACH, 0, -1) for s in (1, -1)]
+            [message(far.at[b], side.at[0, b], 0, 1), message(far.at[b], side.at[1, b], 0, -1)]
+            for b in range(FAR)
         ]
 
-    def side_messages(far, side):
-        return [message(far, side.at[0], 0, 1), message(far, side.at[1], 0, -1)]
-
-    msg_c = [rim_messages(n, lv[n]["c"], lv[n]["spc"], lv[n]["rpc"], RIM[n]) for n in range(3)]
-    msg_t = [rim_messages(n, lv[n]["t"], lv[n]["spt"], lv[n]["rpt"], RIM[n] - 1) for n in range(3)]
-    msg_fc, msg_ft = far_messages(None, far_c), far_messages(None, far_t)
+    c0, t0, raw = lv[0]["c"], lv[0]["t"], lv[0]["raw"]
+    msg_c = [rim_messages(n, lv[n]["c"], lv[n]["spc"], lv[n]["rpc"], RIM[n], 0) for n in range(3)]
+    msg_t = [
+        rim_messages(
+            n, lv[n]["t"] if n > 0 else raw, lv[n]["spt"], lv[n]["rpt"], RIM[n] - 1, 2 * (n == 1)
+        )
+        for n in range(3)
+    ]
+    msg_fc, msg_ft = far_messages(far_c), far_messages(far_t)
     msg_sc, msg_st = side_messages(far_c, side_c), side_messages(far_t, side_t)
-    every = sum(msg_c + msg_t, []) + msg_fc + msg_ft + msg_sc + msg_st
+    every = sum(msg_c + msg_t + msg_sc + msg_st, []) + list(msg_fc.values()) + list(msg_ft.values())
 
     own0 = pl.ds(RIM[0], OX[0])
     loads = []
@@ -296,7 +300,7 @@
         kk = (k % 2) * 8 + k // 2
         loads.append((v_ref.at[k], lv[0]["c"].at[own0, kk, pl.ds(0, 256)]))
         for n in range(2):
-            loads.append((m_ref.at[n, k], lv[0]["t"].at[own0, 16 * n + kk, pl.ds(0, 256)]))
+            loads.append((m_ref.at[n, k], raw.at[own0, 16 * n + kk, pl.ds(0, 256)]))
     loads += [(f_ref, fr), (i_ref, ic), (b_ref, gr)]
     loads = [pltpu.make_async_copy(s, d, in_sem.at[n]) for n, (s, d) in enumerate(loads)]
     for load in loads:
@@ -323,20 +327,14 @@
     for load in loads:
         load.wait()
 
-    c0, t0 = lv[0]["c"], lv[0]["t"]
     ic_f = ic[...].astype(jnp.float32)
     ic_f = ic_f.reshape(OX[0], 1, 256)
     dr_f = (fr[...] * gr[...].astype(jnp.float32)).reshape(OX[0], 1, 256)
     sub = lax.broadcasted_iota(jnp.int32, (OX[0], 8, 256), 1)
     c0[own0, 16:24, 0:256] = jnp.where(sub == 0, ic_f, jnp.where(sub == 1, dr_f, 0.0))
 
-    pl.semaphore_wait(barrier, arrivals)
-    for one in msg_c[0][:2] + msg_t[0][:2]:
-        one.start()
-    pack_columns(0, c0, lv[0]["spc"], 24)
-    pack_columns(0, t0, lv[0]["spt"], 32)
-    for one in msg_c[0][2:] + msg_t[0][2:]:
-        one.start()
+    pack_columns(0, c0, lv[0]["spc"], 24, range(OX[0]), 0)
+    pack_columns(0, raw, lv[0]["spt"], 32, range(OX[0]), 0)
 
     for level in range(3):
         rim, own, width = RIM[level], OX[level + 1], max(OY[level], 128)
@@ -347,56 +345,70 @@
         if level < 2:
             target = lv[level + 1]["c"]
             target[RIM[level + 1] : RIM[level + 1] + own, :, 0:128] = coarse
-            for one in msg_c[level + 1][:2]:
-                one.start()
-            pack_columns(level + 1, target, lv[level + 1]["spc"], 24)
-            for one in msg_c[level + 1][2:]:
-                one.start()
+            pack_columns(level + 1, target, lv[level + 1]["spc"], 24, range(own), 0)
         else:
             far_c[REACH] = sum(roll(coarse[k], 32 * k, 1) for k in range(4))
-            for one in msg_fc:
-                one.start()
+
+    pl.semaphore_wait(barrier, arrivals)
+    for one in msg_c[0][2:4] + msg_t[0][2:4] + msg_c[0][:2] + msg_t[0][:2]:
+        one.start()
+    for one in msg_c[0][4:] + msg_t[0][4:] + msg_c[1] + msg_c[2] + list(msg_fc.values()):
+        one.start()
+    for one in msg_sc[REACH]:
+        one.start()
 
     def refs(level):
         return [lv[level][key] for key in ("e", "y4", "z", "r", "t")]
 
-    def gather(level, kind, messages, landed, planes, reach):
-        for one in messages:
-            one.arrived()
-        if OY[level] < 128:
+    def gather(level, kind, messages, planes, reach, sides):
+        landed = lv[level]["rp" + kind]
+        array = raw if (level, kind) == (0, "t") else lv[level][kind]
+        for side in sides:
+            which = {0: messages[2:4], -1: messages[1:2] + messages[4:6], 1: messages[0:1] + messages[6:8]}
+            for one in which[side]:
+                one.arrived()
+        if OY[level] < 128 and 0 in sides:
             for one in messages[:2]:
                 one.sent()
-        unpack_columns(level, lv[level][kind], lv[level][landed], planes, reach)
-
-    def first_sweep(level, rows, factor):
+        for side in sides:
+            unpack_columns(level, array, landed, planes, reach, side)
+
+    def first_sweep(level, low, high):
         t = lv[level]["t"]
+        source, factor = (raw, lv[0]["r"]) if level == 0 else (t, lv[level]["q"])
 
         def body(i):
-            t[i] = t[i] * factor[i]
-
-        over_rows(RIM[level] - rows, OX[level] + 2 * rows, body, 4)
-
-    def sweep(level, src, dst, rows):
+            t[i] = source[i] * factor[i]
+
+        over_rows(RIM[level] + low, high - low, body, min(4, high - low))
+
+    def sweep_range(level, src, dst, low, high):
         args = refs(level)
 
         over_rows(
-            RIM[level] - rows,
-            OX[level] + 2 * rows,
+            RIM[level] + low,
+            high - low,
             lambda i: sweep_row(src, dst, *args, i),
             UNROLL[level],
         )
 
-    def restricted_remainder(level, src):
+    def sweep(level, src, dst, rows):
+        sweep_range(level, src, dst, -rows, OX[level] + rows)
+
+    def restricted_remainder(level, src, ranges):
         args = refs(level)
-        width, own = max(OY[level], 128), OX[level + 1]
+        width = max(OY[level], 128)
 
         def body(n):
             i = RIM[level] + 2 * n
             pair = [remainder_row(src, *args, lv[level]["g"], i + k, width) for k in range(2)]
             rest[n, :, 0:width] = pair[0] + pair[1]
 
-        over_rows(0, own, body, UNROLL_R[level])
-        block = rest[0:own, :, 0:width].reshape(own * 32, width)
+        for low, high in ranges:
+            over_rows(low, high - low, body, UNROLL_R[level])
+        block = jnp.concatenate([rest[low:high, :, 0:width] for low, high in ranges], 0)
+        own = block.shape[0]
+        block = block.reshape(own * 32, width)
         return exact_dot(block, restrict_matrix(level)).reshape(own, 32, 128)
 
     def prolonged(level, src, dst, rows):
@@ -415,71 +427,105 @@
 
         over_rows(0, n, body, 2)
 
-    gather(0, "c", msg_c[0], "rpc", 24, RIM[0])
-    coefficients(0, c0, *[lv[0][k] for k in ("e", "y4", "z")], None, lv[0]["r"], lv[0]["g"], 3)
-    gather(0, "t", msg_t[0], "rpt", 32, RIM[0] - 1)
-    for one in msg_t[0][:2]:
-        one.sent()
-    first_sweep(0, 3, lv[0]["r"])
-    sweep(0, t0, lv[0]["a"], 2)
-    t_next = restricted_remainder(0, lv[0]["a"])
+    def all_coefficients(level, low, high):
+        refs_c = [lv[level].get(k) for k in ("c", "e", "y4", "z", "q", "r", "g")]
+        coefficients(level, *refs_c, low, high)
+
+    n0, h0 = OX[0], RIM[0] - 1
+    gather(0, "c", msg_c[0], 24, RIM[0], (0,))
+    gather(0, "t", msg_t[0], 32, h0, (0,))
+    all_coefficients(0, 1, n0 - 1)
+    first_sweep(0, 1, n0 - 1)
+    sweep_range(0, t0, lv[0]["a"], 2, n0 - 2)
+    gather(0, "c", msg_c[0], 24, RIM[0], (-1, 1))
+    gather(0, "t", msg_t[0], 32, h0, (-1, 1))
+    for low, high in ((-h0, 1), (n0 - 1, n0 + h0)):
+        all_coefficients(0, low, high)
+        first_sweep(0, low, high)
+    for low, high in ((1 - h0, 2), (n0 - 2, n0 + h0 - 1)):
+        sweep_range(0, t0, lv[0]["a"], low, high)
+
+    t1, h1, n1 = lv[1]["t"], RIM[1] - 1, OX[1]
+    own1 = restricted_remainder(0, lv[0]["a"], [(0, h1), (n1 - h1, n1)])
+    t1[RIM[1] : RIM[1] + h1, :, 0:128] = own1[:h1]
+    t1[RIM[1] + n1 - h1 : RIM[1] + n1, :, 0:128] = own1[h1:]
+    for one in msg_t[1][:2]:
+        one.start()
+    ends = [*range(h1), *range(n1 - h1, n1)]
+    pack_columns(1, t1, lv[1]["spt"], 32, ends, 2)
+    for one in msg_t[1][4:]:
+        one.start()
+    t1[RIM[1] + h1 : RIM[1] + n1 - h1, :, 0:128] = restricted_remainder(
+        0, lv[0]["a"], [(h1, n1 - h1)]
+    )
+    pack_columns(1, t1, lv[1]["spt"], 32, range(h1, n1 - h1), 0, 2)
+    for one in msg_t[1][2:4]:
+        one.start()
 
     for level in (1, 2):
-        t = lv[level]["t"]
-        t[RIM[level] : RIM[level] + OX[level], :, 0:128] = t_next
-        for one in msg_t[level][:2]:
-            one.start()
-        pack_columns(level, t, lv[level]["spt"], 32)
-        for one in msg_t[level][2:]:
-            one.start()
-        gather(level, "c", msg_c[level], "rpc", 24, RIM[level])
-        coefficients(
-            level, *[lv[level][k] for k in ("c", "e", "y4", "z", "q", "r", "g")], RIM[level] - 1
-        )
+        t, own, h = lv[level]["t"], OX[level], RIM[level] - 1
+        if level == 2:
+            t[RIM[2] : RIM[2] + own, :, 0:128] = restricted_remainder(1, lv[1]["a"], [(0, own)])
+            for one in msg_t[2][:2]:
+                one.start()
+            pack_columns(2, t, lv[2]["spt"], 32, range(own), 0)
+            for one in msg_t[2][4:] + msg_t[2][2:4]:
+                one.start()
+        gather(level, "c", msg_c[level], 24, RIM[level], (0, -1, 1))
+        all_coefficients(level, -h, own + h)
         if level == 1:
-            for one in msg_fc:
-                one.arrived()
-            for one in msg_sc:
-                one.start()
-        gather(level, "t", msg_t[level], "rpt", 32, RIM[level] - 1)
-        if OY[level] >= 128:
-            for one in msg_t[level][:2]:
-                one.sent()
-        first_sweep(level, RIM[level] - 1, lv[level]["q"])
-        sweep(level, t, lv[level]["a"], RIM[level] - 2)
-        t_next = restricted_remainder(level, lv[level]["a"])
-
+            for d in range(1, REACH + 1):
+                for s in (d, -d):
+                    msg_fc[s].arrived()
+                    for one in msg_sc[REACH - s]:
+                        one.start()
+        gather(level, "t", msg_t[level], 32, h, (0,))
+        for one in [] if OY[level] < 128 else msg_t[level][:2]:
+            one.sent()
+        first_sweep(level, 0, own)
+        sweep_range(level, t, lv[level]["a"], 1, own - 1)
+        gather(level, "t", msg_t[level], 32, h, (-1, 1))
+        first_sweep(level, -h, 0)
+        first_sweep(level, own, own + h)
+        sweep_range(level, t, lv[level]["a"], 1 - h, 1)
+        sweep_range(level, t, lv[level]["a"], own - 1, own + h - 1)
+
+    t_next = restricted_remainder(2, lv[2]["a"], [(0, OX[3])])
     far_t[REACH] = sum(roll(t_next[k], 32 * k, 1) for k in range(4))
-    for one in msg_ft:
+    for one in list(msg_ft.values()) + msg_st[REACH]:
         one.start()
 
-    def unpack_far(dest, far, side, planes):
+    def unpack_far(dest, far, side, planes, factor):
         lane = lane_iota(planes)
 
-        def body(b, _):
+        def body(b):
             own, left, right = far[b], side[0, b], side[1, b]
             for k in range(4):
                 tile = jnp.where(lane < 32, roll(own, -32 * k, 1), 0.0)
                 tile = jnp.where((lane >= 32) & (lane < 64), roll(right, 32 - 32 * k, 1), tile)
                 tile = jnp.where(lane >= 96, roll(left, 96 - 32 * k, 1), tile)
-                dest[4 * b + k] = tile
-            return 0
-
-        lax.fori_loop(0, FAR, body, 0)
-
-    for one in msg_sc:
-        one.arrived()
-    unpack_far(lv[3]["c"], far_c, side_c, 24)
-    coefficients(3, *[lv[3][k] for k in ("c", "e", "y4", "z", "q", "r")], None, RIM[3] - 1)
-    for one in msg_ft:
-        one.arrived()
-    for one in msg_st:
-        one.start()
-    for one in msg_st:
-        one.arrived()
+                dest[4 * b + k] = tile if factor is None else tile * factor[4 * b + k]
+
+        over_rows(0, FAR, body, 2)
+
+    for pair in msg_sc:
+        for one in pair:
+            one.arrived()
+    q3 = lv[3]["q"]
+    unpack_far(lv[3]["c"], far_c, side_c, 24, None)
+    all_coefficients(3, 1 - RIM[3], OX[3] + RIM[3] - 1)
+    q3[0] = q3[1]
+    q3[OX[3] + 2 * RIM[3] - 1] = q3[1]
+    for d in range(1, REACH + 1):
+        for s in (d, -d):
+            msg_ft[s].arrived()
+            for one in msg_st[REACH - s]:
+                one.start()
+    for pair in msg_st:
+        for one in pair:
+            one.arrived()
     t3, a3, b3 = lv[3]["t"], lv[3]["a"], lv[3]["b"]
-    unpack_far(t3, far_t, side_t, 32)
-    first_sweep(3, RIM[3] - 1, lv[3]["q"])
+    unpack_far(t3, far_t, side_t, 32, q3)
     args3 = refs(3)
 
     def coarse_sweep(src, dst, s):
@@ -526,7 +572,7 @@
                 )
                 store.start()
                 stores.append(store)
-    waited = msg_t[0][:2] + msg_t[1][:2] + msg_t[2][:2] + msg_c[2][:2]
+    waited = msg_t[1][:2] + msg_t[2][:2] + msg_c[2][:2]
     for one in every:
         if one not in waited:
             one.sent()
@@ -545,7 +591,9 @@
         planes += [32] if level < 3 else []
         scratch += [pltpu.VMEM((rows, p, lanes), f32) for p in planes]
         if level < 3:
-            scratch += [pltpu.VMEM((n, p, 128), f32) for p in (24, 32) for n in (2, 6)]
+            scratch += [pltpu.VMEM((n, p, 128), f32) for p in (24, 32) for n in (4, 6)]
+        if level == 0:
+            scratch += [pltpu.VMEM((rows, 32, lanes), f32)]
     scratch += [pltpu.VMEM((16, 32, 256), f32)]
     scratch += [pltpu.VMEM((FAR, 24, 128), f32), pltpu.VMEM((FAR, 32, 128), f32)]
     scratch += [pltpu.VMEM((2, FAR, 24, 128), f32), pltpu.VMEM((2, FAR, 32, 128), f32)]
@@ -554,7 +602,7 @@
         pltpu.VMEM((32, 256), jnp.int32),
         pltpu.VMEM((32, 256), jnp.int32),
     ]
-    messages = 6 * 8 + 4 * REACH + 4
+    messages = 6 * 8 + 4 * REACH + 4 * FAR
     scratch += [pltpu.SemaphoreType.DMA((51,)), pltpu.SemaphoreType.DMA((64,))]
     scratch += [pltpu.SemaphoreType.DMA((messages,)), pltpu.SemaphoreType.DMA((messages,))]
 

time: 80.4 us -> 75.3 us (0.937)
  Pallas kernels: 77.6 us -> 72.8 us
    pallas_call x1, Pallas kernels: 77.6 us -> 72.8 us  [per_device(): pl.pallas_call(functools.partial(kernel, nx, ny), out_shape=jax.ShapeDtyp...]
where the time goes in v3:
time: 75.3 us; the launch traced here: 75.1 us
  Pallas kernels  72.8 us (97%)
  local copies, waits for them, and re-layouts  2.31 us (3%)
    pallas_call x1, Pallas kernels, per_device(): pl.pallas_call(functools.partial(kernel, nx, ny), out_shape=jax.ShapeDtyp...  72.8 us
    unnamed x1, local copies, waits for them, and re-layouts  2.31 us

profile of v3, /device:TPU:5, one launch (start us, length us, event | category | flops | bytes accessed | tf_op | source)
XLA Modules:
  0.0 75.1 jit_solution(2799889832815945571)
XLA Ops:
  0.0 72.8 %shard_map.55 = f32[2,16,32,256]{3,2,1,0:T(8,128)} custom-call(f32[2,16,32,256]{3,2,1,0:T(8,128)} %m_ref.1, f32[16,32,256]{2,1,0:T(8,128)} %v_ref.1, f32[32,256]{1,0:T(8,128)} %f_ref.1, s32[32,256]{1,0:T(8,128)} %i_ref.1, s32[32,256]{1,0:T(8,128)} %b_ref.1), custom_call_target="tpu_custom_call" | custom-call | tf_op jit(solution)/shard_map/pallas_call | solution.py:610
  72.8 2.3 %copy.7 = f32[2,16,32,256]{3,2,1,0:T(8,128)} copy(f32[2,16,32,256]{3,2,1,0:T(8,128)} %shard_map.55) | data formatting | bytes 2097152

commit v4 on v3

--- a/solution.py
+++ b/solution.py
@@ -22,6 +22,7 @@
 UNROLL = (2, 3, 6, 8)
 UNROLL_C = (2, 3, 6, 5)
 UNROLL_R = (1, 2, 4)
+DIRECT = 6
 REACH = 6
 FAR = 2 * REACH + 1
 SIDES = ((0, -1), (0, 1), (-1, -1), (-1, 1), (1, -1), (1, 1))
@@ -81,10 +82,12 @@
 class Message:
     def __init__(self, place, sems, index, src, dst, dx, dy):
         gx, gy, nx, ny = place
+        self.way = (dx, dy)
         self.to_there = (gx + dx >= 0) & (gx + dx < nx) & (gy + dy >= 0) & (gy + dy < ny)
         self.from_there = (gx - dx >= 0) & (gx - dx < nx) & (gy - dy >= 0) & (gy - dy < ny)
         target = (jnp.clip(gx + dx, 0, nx - 1), jnp.clip(gy + dy, 0, ny - 1))
         self.dst = dst
+        self.pending = []
         self.copy = pltpu.make_async_remote_copy(
             src_ref=src,
             dst_ref=dst,
@@ -94,42 +97,74 @@
             device_id_type=MESH,
         )
 
-    def clear(self):
-        @pl.when(jnp.logical_not(self.from_there))
-        def _():
-            self.dst[...] = jnp.zeros(self.dst.shape, self.dst.dtype)
-
-    def start(self):
-        @pl.when(self.to_there)
-        def _():
-            self.copy.start()
-
-    def arrived(self):
-        @pl.when(self.from_there)
-        def _():
-            self.copy.wait_recv()
-
-    def sent(self):
-        @pl.when(self.to_there)
-        def _():
-            self.copy.wait_send()
-
-
-def pack_columns(level, source, dest, planes, rows, base, start=None):
+
+def by_way(messages):
+    groups = {}
+    for one in messages:
+        groups.setdefault(one.way, []).append(one)
+    return groups.values()
+
+
+def clear(messages):
+    for group in by_way(messages):
+
+        @pl.when(jnp.logical_not(group[0].from_there))
+        def _(group=group):
+            for one in group:
+                one.dst[...] = jnp.zeros(one.dst.shape, one.dst.dtype)
+
+
+def start(messages):
+    for group in by_way(messages):
+
+        @pl.when(group[0].to_there)
+        def _(group=group):
+            for one in group:
+                one.copy.start()
+
+    for one in messages:
+        one.pending = ["arrived", "sent"]
+
+
+def arrived(messages):
+    for group in by_way(messages):
+
+        @pl.when(group[0].from_there)
+        def _(group=group):
+            for one in group:
+                one.copy.wait_recv()
+
+    for one in messages:
+        one.pending.remove("arrived")
+
+
+def sent(messages):
+    for group in by_way(messages):
+
+        @pl.when(group[0].to_there)
+        def _(group=group):
+            for one in group:
+                one.copy.wait_send()
+
+    for one in messages:
+        one.pending.remove("sent")
+
+
+def pack_columns(level, source, dest, planes):
     w, rim = PW[level], RIM[level]
     lane = lane_iota(planes)
     tile = (OY[level] - 1) // 128
     edge = (OY[level] - w) % 128
     zero = jnp.zeros((planes, 128), jnp.float32)
-    left, right = (zero, zero) if start is None else (dest[start], dest[start + 1])
-    for i in rows:
+    left, right = zero, zero
+    for i in range(OX[level]):
         here = (lane >= w * i) & (lane < w * i + w)
         a = source[rim + i, :, 0:128]
         b = source[rim + i, :, tile * 128 : tile * 128 + 128]
         left = jnp.where(here, roll(a, w * i, 1), left)
         right = jnp.where(here, roll(b, w * i - edge, 1), right)
-    dest[base] = left
-    dest[base + 1] = right
+    dest[0] = left
+    dest[1] = right
 
 
 def unpack_columns(level, dest, packs, planes, reach, side):
@@ -256,7 +291,7 @@
     def message(src, dst, dx, dy):
         return Message(place, sems, next(count), src, dst, dx, dy)
 
-    def rim_messages(level, array, packs, landed, reach, corner):
+    def rim_messages(level, array, packs, landed, reach):
         rim, own = RIM[level], OX[level]
         lanes = pl.ds(0, max(OY[level], 128))
         out = [
@@ -268,31 +303,66 @@
                 array.at[pl.ds(rim - reach, reach), :, lanes], 1, 0),
         ]
         for slot, (dx, dy) in enumerate(SIDES):
-            pack = (0 if dy > 0 else 1) + (corner if dx != 0 else 0)
-            out.append(message(packs.at[pack], landed.at[slot], -dx, -dy))
+            out.append(message(packs.at[0 if dy > 0 else 1], landed.at[slot], -dx, -dy))
         return out
 
-    def far_messages(far):
-        order = [k * s for k in range(REACH, 0, -1) for s in (1, -1)]
-        return {d: message(far.at[REACH], far.at[REACH - d], d, 0) for d in order}
+    def far_messages(far, side):
+        out = []
+        for d in [k * s for k in range(REACH, 0, -1) for s in (1, -1)]:
+            out.append(message(far.at[REACH], far.at[REACH - d], d, 0))
+            for n in range(2 if abs(d) > DIRECT else 0):
+                out.append(message(far.at[REACH], side.at[n, REACH - d], d, 1 - 2 * n))
+        return out
 
     def side_messages(far, side):
-        return [
-            [message(far.at[b], side.at[0, b], 0, 1), message(far.at[b], side.at[1, b], 0, -1)]
-            for b in range(FAR)
-        ]
+        near = pl.ds(REACH - DIRECT, 2 * DIRECT + 1)
+        whole = [message(far.at[near], side.at[n, near], 0, 1 - 2 * n) for n in range(2)]
+        first = next(count) - 2
+        blocks = {
+            b: [
+                Message(place, sems, first + n, far.at[b], side.at[n, b], 0, 1 - 2 * n)
+                for n in range(2)
+            ]
+            for b in range(REACH - DIRECT, REACH + DIRECT + 1)
+        }
+        return whole, blocks
+
+    def pass_on(far, side):
+        for d in range(1, DIRECT + 1):
+            for s in (d, -d):
+                arrived([one for one in far if one.way == (s, 0)])
+                start(side[REACH - s])
 
     c0, t0, raw = lv[0]["c"], lv[0]["t"], lv[0]["raw"]
-    msg_c = [rim_messages(n, lv[n]["c"], lv[n]["spc"], lv[n]["rpc"], RIM[n], 0) for n in range(3)]
+    msg_c = [rim_messages(n, lv[n]["c"], lv[n]["spc"], lv[n]["rpc"], RIM[n]) for n in range(3)]
     msg_t = [
         rim_messages(
-            n, lv[n]["t"] if n > 0 else raw, lv[n]["spt"], lv[n]["rpt"], RIM[n] - 1, 2 * (n == 1)
+            n, lv[n]["t"] if n > 0 else raw, lv[n]["spt"], lv[n]["rpt"], RIM[n] - 1
         )
         for n in range(3)
     ]
-    msg_fc, msg_ft = far_messages(far_c), far_messages(far_t)
-    msg_sc, msg_st = side_messages(far_c, side_c), side_messages(far_t, side_t)
-    every = sum(msg_c + msg_t + msg_sc + msg_st, []) + list(msg_fc.values()) + list(msg_ft.values())
+    msg_fc, msg_ft = far_messages(far_c, side_c), far_messages(far_t, side_t)
+    all_sc, msg_sc = side_messages(far_c, side_c)
+    all_st, msg_st = side_messages(far_t, side_t)
+    every = sum(msg_c + msg_t, []) + msg_fc + msg_ft + all_sc + all_st
+
+    barrier = pltpu.get_barrier_semaphore()
+    far_away = [d for d in range(-REACH, REACH + 1) if abs(d) > DIRECT]
+    partners = [(d, 0) for d in range(-REACH, REACH + 1) if d != 0] + list(SIDES)
+    partners += [(d, s) for d in far_away for s in (-1, 1)]
+    arrivals = 0
+    for dx, dy in partners:
+        there = (gx + dx >= 0) & (gx + dx < nx) & (gy + dy >= 0) & (gy + dy < ny)
+        arrivals = arrivals + there.astype(jnp.int32)
+
+        @pl.when(there)
+        def _(dx=dx, dy=dy):
+            pl.semaphore_signal(
+                barrier,
+                inc=1,
+                device_id=(jnp.clip(gx + dx, 0, nx - 1), jnp.clip(gy + dy, 0, ny - 1)),
+                device_id_type=MESH,
+            )
 
     own0 = pl.ds(RIM[0], OX[0])
     loads = []
@@ -306,24 +376,7 @@
     for load in loads:
         load.start()
 
-    barrier = pltpu.get_barrier_semaphore()
-    partners = [(d, 0) for d in range(-REACH, REACH + 1) if d != 0] + list(SIDES)
-    arrivals = 0
-    for dx, dy in partners:
-        there = (gx + dx >= 0) & (gx + dx < nx) & (gy + dy >= 0) & (gy + dy < ny)
-        arrivals = arrivals + there.astype(jnp.int32)
-
-        @pl.when(there)
-        def _(dx=dx, dy=dy):
-            pl.semaphore_signal(
-                barrier,
-                inc=1,
-                device_id=(jnp.clip(gx + dx, 0, nx - 1), jnp.clip(gy + dy, 0, ny - 1)),
-                device_id_type=MESH,
-            )
-
-    for one in every:
-        one.clear()
+    clear(every)
     for load in loads:
         load.wait()
 
@@ -333,8 +386,12 @@
     sub = lax.broadcasted_iota(jnp.int32, (OX[0], 8, 256), 1)
     c0[own0, 16:24, 0:256] = jnp.where(sub == 0, ic_f, jnp.where(sub == 1, dr_f, 0.0))
 
-    pack_columns(0, c0, lv[0]["spc"], 24, range(OX[0]), 0)
-    pack_columns(0, raw, lv[0]["spt"], 32, range(OX[0]), 0)
+    pack_columns(0, c0, lv[0]["spc"], 24)
+    pack_columns(0, raw, lv[0]["spt"], 32)
+
+    pl.semaphore_wait(barrier, arrivals)
+    start(msg_c[0][2:4] + msg_t[0][2:4])
+    start(msg_c[0][:2] + msg_t[0][:2] + msg_c[0][4:] + msg_t[0][4:])
 
     for level in range(3):
         rim, own, width = RIM[level], OX[level + 1], max(OY[level], 128)
@@ -345,17 +402,9 @@
         if level < 2:
             target = lv[level + 1]["c"]
             target[RIM[level + 1] : RIM[level + 1] + own, :, 0:128] = coarse
-            pack_columns(level + 1, target, lv[level + 1]["spc"], 24, range(own), 0)
+            pack_columns(level + 1, target, lv[level + 1]["spc"], 24)
         else:
             far_c[REACH] = sum(roll(coarse[k], 32 * k, 1) for k in range(4))
-
-    pl.semaphore_wait(barrier, arrivals)
-    for one in msg_c[0][2:4] + msg_t[0][2:4] + msg_c[0][:2] + msg_t[0][:2]:
-        one.start()
-    for one in msg_c[0][4:] + msg_t[0][4:] + msg_c[1] + msg_c[2] + list(msg_fc.values()):
-        one.start()
-    for one in msg_sc[REACH]:
-        one.start()
 
     def refs(level):
         return [lv[level][key] for key in ("e", "y4", "z", "r", "t")]
@@ -365,11 +414,9 @@
         array = raw if (level, kind) == (0, "t") else lv[level][kind]
         for side in sides:
             which = {0: messages[2:4], -1: messages[1:2] + messages[4:6], 1: messages[0:1] + messages[6:8]}
-            for one in which[side]:
-                one.arrived()
+            arrived(which[side])
         if OY[level] < 128 and 0 in sides:
-            for one in messages[:2]:
-                one.sent()
+            sent(messages[:2])
         for side in sides:
             unpack_columns(level, array, landed, planes, reach, side)
 
@@ -395,7 +442,7 @@
     def sweep(level, src, dst, rows):
         sweep_range(level, src, dst, -rows, OX[level] + rows)
 
-    def restricted_remainder(level, src, ranges):
+    def remainder_rows(level, src, low, high):
         args = refs(level)
         width = max(OY[level], 128)
 
@@ -404,11 +451,11 @@
             pair = [remainder_row(src, *args, lv[level]["g"], i + k, width) for k in range(2)]
             rest[n, :, 0:width] = pair[0] + pair[1]
 
-        for low, high in ranges:
-            over_rows(low, high - low, body, UNROLL_R[level])
-        block = jnp.concatenate([rest[low:high, :, 0:width] for low, high in ranges], 0)
-        own = block.shape[0]
-        block = block.reshape(own * 32, width)
+        over_rows(low, high - low, body, min(UNROLL_R[level], high - low))
+
+    def restricted(level):
+        width, own = max(OY[level], 128), OX[level + 1]
+        block = rest[0:own, :, 0:width].reshape(own * 32, width)
         return exact_dot(block, restrict_matrix(level)).reshape(own, 32, 128)
 
     def prolonged(level, src, dst, rows):
@@ -435,8 +482,10 @@
     gather(0, "c", msg_c[0], 24, RIM[0], (0,))
     gather(0, "t", msg_t[0], 32, h0, (0,))
     all_coefficients(0, 1, n0 - 1)
+    start(msg_c[1] + msg_c[2])
     first_sweep(0, 1, n0 - 1)
     sweep_range(0, t0, lv[0]["a"], 2, n0 - 2)
+    remainder_rows(0, lv[0]["a"], 2, OX[1] - 2)
     gather(0, "c", msg_c[0], 24, RIM[0], (-1, 1))
     gather(0, "t", msg_t[0], 32, h0, (-1, 1))
     for low, high in ((-h0, 1), (n0 - 1, n0 + h0)):
@@ -444,44 +493,25 @@
         first_sweep(0, low, high)
     for low, high in ((1 - h0, 2), (n0 - 2, n0 + h0 - 1)):
         sweep_range(0, t0, lv[0]["a"], low, high)
-
-    t1, h1, n1 = lv[1]["t"], RIM[1] - 1, OX[1]
-    own1 = restricted_remainder(0, lv[0]["a"], [(0, h1), (n1 - h1, n1)])
-    t1[RIM[1] : RIM[1] + h1, :, 0:128] = own1[:h1]
-    t1[RIM[1] + n1 - h1 : RIM[1] + n1, :, 0:128] = own1[h1:]
-    for one in msg_t[1][:2]:
-        one.start()
-    ends = [*range(h1), *range(n1 - h1, n1)]
-    pack_columns(1, t1, lv[1]["spt"], 32, ends, 2)
-    for one in msg_t[1][4:]:
-        one.start()
-    t1[RIM[1] + h1 : RIM[1] + n1 - h1, :, 0:128] = restricted_remainder(
-        0, lv[0]["a"], [(h1, n1 - h1)]
-    )
-    pack_columns(1, t1, lv[1]["spt"], 32, range(h1, n1 - h1), 0, 2)
-    for one in msg_t[1][2:4]:
-        one.start()
+    for low, high in ((0, 2), (OX[1] - 2, OX[1])):
+        remainder_rows(0, lv[0]["a"], low, high)
 
     for level in (1, 2):
         t, own, h = lv[level]["t"], OX[level], RIM[level] - 1
         if level == 2:
-            t[RIM[2] : RIM[2] + own, :, 0:128] = restricted_remainder(1, lv[1]["a"], [(0, own)])
-            for one in msg_t[2][:2]:
-                one.start()
-            pack_columns(2, t, lv[2]["spt"], 32, range(own), 0)
-            for one in msg_t[2][4:] + msg_t[2][2:4]:
-                one.start()
+            remainder_rows(1, lv[1]["a"], 0, own)
+        t[RIM[level] : RIM[level] + own, :, 0:128] = restricted(level - 1)
+        start(msg_t[level][:2])
+        pack_columns(level, t, lv[level]["spt"], 32)
+        start(msg_t[level][4:] + msg_t[level][2:4])
+        if level == 2:
+            pass_on(msg_fc, msg_sc)
         gather(level, "c", msg_c[level], 24, RIM[level], (0, -1, 1))
         all_coefficients(level, -h, own + h)
-        if level == 1:
-            for d in range(1, REACH + 1):
-                for s in (d, -d):
-                    msg_fc[s].arrived()
-                    for one in msg_sc[REACH - s]:
-                        one.start()
         gather(level, "t", msg_t[level], 32, h, (0,))
-        for one in [] if OY[level] < 128 else msg_t[level][:2]:
-            one.sent()
+        if OY[level] >= 128:
+            sent(msg_t[level][:2])
+            start(msg_fc + msg_sc[REACH])
         first_sweep(level, 0, own)
         sweep_range(level, t, lv[level]["a"], 1, own - 1)
         gather(level, "t", msg_t[level], 32, h, (-1, 1))
@@ -490,10 +520,10 @@
         sweep_range(level, t, lv[level]["a"], 1 - h, 1)
         sweep_range(level, t, lv[level]["a"], own - 1, own + h - 1)
 
-    t_next = restricted_remainder(2, lv[2]["a"], [(0, OX[3])])
+    remainder_rows(2, lv[2]["a"], 0, OX[3])
+    t_next = restricted(2)
     far_t[REACH] = sum(roll(t_next[k], 32 * k, 1) for k in range(4))
-    for one in list(msg_ft.values()) + msg_st[REACH]:
-        one.start()
+    start(msg_ft + msg_st[REACH])
 
     def unpack_far(dest, far, side, planes, factor):
         lane = lane_iota(planes)
@@ -508,22 +538,17 @@
 
         over_rows(0, FAR, body, 2)
 
-    for pair in msg_sc:
-        for one in pair:
-            one.arrived()
+    for one in all_sc + all_st:
+        one.pending = ["arrived", "sent"]
+    arrived(all_sc + [one for one in msg_fc if "arrived" in one.pending])
     q3 = lv[3]["q"]
     unpack_far(lv[3]["c"], far_c, side_c, 24, None)
     all_coefficients(3, 1 - RIM[3], OX[3] + RIM[3] - 1)
     q3[0] = q3[1]
     q3[OX[3] + 2 * RIM[3] - 1] = q3[1]
-    for d in range(1, REACH + 1):
-        for s in (d, -d):
-            msg_ft[s].arrived()
-            for one in msg_st[REACH - s]:
-                one.start()
-    for pair in msg_st:
-        for one in pair:
-            one.arrived()
+    pass_on(msg_ft, msg_st)
+    sent([one for one in every if one.pending == ["sent"]])
+    arrived([one for one in msg_ft if "arrived" in one.pending] + all_st)
     t3, a3, b3 = lv[3]["t"], lv[3]["a"], lv[3]["b"]
     unpack_far(t3, far_t, side_t, 32, q3)
     args3 = refs(3)
@@ -572,10 +597,7 @@
                 )
                 store.start()
                 stores.append(store)
-    waited = msg_t[1][:2] + msg_t[2][:2] + msg_c[2][:2]
-    for one in every:
-        if one not in waited:
-            one.sent()
+    sent([one for one in every if one.pending])
     for store in stores:
         store.wait()
 
@@ -591,7 +613,7 @@
         planes += [32] if level < 3 else []
         scratch += [pltpu.VMEM((rows, p, lanes), f32) for p in planes]
         if level < 3:
-            scratch += [pltpu.VMEM((n, p, 128), f32) for p in (24, 32) for n in (4, 6)]
+            scratch += [pltpu.VMEM((n, p, 128), f32) for p in (24, 32) for n in (2, 6)]
         if level == 0:
             scratch += [pltpu.VMEM((rows, 32, lanes), f32)]
     scratch += [pltpu.VMEM((16, 32, 256), f32)]
@@ -602,7 +624,7 @@
         pltpu.VMEM((32, 256), jnp.int32),
         pltpu.VMEM((32, 256), jnp.int32),
     ]
-    messages = 6 * 8 + 4 * REACH + 4 * FAR
+    messages = 6 * 8 + 4 * REACH + 8 * (REACH - DIRECT) + 8
     scratch += [pltpu.SemaphoreType.DMA((51,)), pltpu.SemaphoreType.DMA((64,))]
     scratch += [pltpu.SemaphoreType.DMA((messages,)), pltpu.SemaphoreType.DMA((messages,))]
 

time: 75.3 us -> 70.4 us (0.935)
  Pallas kernels: 72.8 us -> 67.5 us
    pallas_call x1, Pallas kernels: 72.8 us -> 67.5 us  [per_device(): pl.pallas_call(functools.partial(kernel, nx, ny), out_shape=jax.ShapeDtyp...]
where the time goes in v4:
time: 70.4 us; the launch traced here: 69.9 us
  Pallas kernels  67.5 us (96%)
  local copies, waits for them, and re-layouts  2.31 us (3%)
    pallas_call x1, Pallas kernels, per_device(): pl.pallas_call(functools.partial(kernel, nx, ny), out_shape=jax.ShapeDtyp...  67.5 us
    unnamed x1, local copies, waits for them, and re-layouts  2.31 us

profile of v4, /device:TPU:5, one launch (start us, length us, event | category | flops | bytes accessed | tf_op | source)
XLA Modules:
  0.0 69.9 jit_solution(16198587526629054773)
XLA Ops:
  0.0 67.5 %shard_map.55 = f32[2,16,32,256]{3,2,1,0:T(8,128)} custom-call(f32[2,16,32,256]{3,2,1,0:T(8,128)} %m_ref.1, f32[16,32,256]{2,1,0:T(8,128)} %v_ref.1, f32[32,256]{1,0:T(8,128)} %f_ref.1, s32[32,256]{1,0:T(8,128)} %i_ref.1, s32[32,256]{1,0:T(8,128)} %b_ref.1), custom_call_target="tpu_custom_call" | custom-call | tf_op jit(solution)/shard_map/pallas_call | solution.py:632
  67.5 2.3 %copy.7 = f32[2,16,32,256]{3,2,1,0:T(8,128)} copy(f32[2,16,32,256]{3,2,1,0:T(8,128)} %shard_map.55) | data formatting | bytes 2097152

commit v5 on v4

--- a/solution.py
+++ b/solution.py
@@ -18,10 +18,10 @@
 LN = (384, 256, 128, 128)
 RIM = (4, 5, 6, 24)
 PW = (4, 8, 16, 32)
-TX = tuple(o + 2 * h for o, h in zip(OX[:3], RIM)) + (58,)
-UNROLL = (2, 3, 6, 8)
-UNROLL_C = (2, 3, 6, 5)
-UNROLL_R = (1, 2, 4)
+TX = tuple(o + 2 * h for o, h in zip(OX[:3], RIM)) + (64,)
+UNROLL = (4, 6, 8, 16)
+UNROLL_C = (4, 4, 6, 10)
+UNROLL_R = (2, 4, 4)
 DIRECT = 6
 REACH = 6
 FAR = 2 * REACH + 1

time: 70.4 us -> 65.3 us (0.928)
  Pallas kernels: 67.5 us -> 62.5 us
    pallas_call x1, Pallas kernels: 67.5 us -> 62.5 us  [per_device(): pl.pallas_call(functools.partial(kernel, nx, ny), out_shape=jax.ShapeDtyp...]
where the time goes in v5:
time: 65.3 us; the launch traced here: 64.8 us
  Pallas kernels  62.5 us (96%)
  local copies, waits for them, and re-layouts  2.31 us (4%)
    pallas_call x1, Pallas kernels, per_device(): pl.pallas_call(functools.partial(kernel, nx, ny), out_shape=jax.ShapeDtyp...  62.5 us
    unnamed x1, local copies, waits for them, and re-layouts  2.31 us

profile of v5, /device:TPU:5, one launch (start us, length us, event | category | flops | bytes accessed | tf_op | source)
XLA Modules:
  0.0 64.8 jit_solution(6138359973680338996)
XLA Ops:
  0.0 62.5 %shard_map.55 = f32[2,16,32,256]{3,2,1,0:T(8,128)} custom-call(f32[2,16,32,256]{3,2,1,0:T(8,128)} %m_ref.1, f32[16,32,256]{2,1,0:T(8,128)} %v_ref.1, f32[32,256]{1,0:T(8,128)} %f_ref.1, s32[32,256]{1,0:T(8,128)} %i_ref.1, s32[32,256]{1,0:T(8,128)} %b_ref.1), custom_call_target="tpu_custom_call" | custom-call | tf_op jit(solution)/shard_map/pallas_call | solution.py:632
  62.5 2.3 %copy.7 = f32[2,16,32,256]{3,2,1,0:T(8,128)} copy(f32[2,16,32,256]{3,2,1,0:T(8,128)} %shard_map.55) | data formatting | bytes 2097152

commit v6 on v5

--- a/solution.py
+++ b/solution.py
@@ -167,15 +167,15 @@
     dest[1] = right
 
 
-def unpack_columns(level, dest, packs, planes, reach, side):
+def unpack_columns(level, dest, packs, planes, reach, side, skip=0):
     w, rim, own = PW[level], RIM[level], OX[level]
     lane = lane_iota(planes)
     last = LN[level] - 128
     start = OY[level] % 128
     row0, count, shift, slot = {
-        -1: (-reach, reach, own - reach, 2),
+        -1: (-reach, reach - skip, own - reach, 2),
         0: (0, own, 0, 0),
-        1: (own, reach, 0, 4),
+        1: (own + skip, reach - skip, skip, 4),
     }[side]
     for i in range(count):
         at = w * (i + shift)
@@ -334,17 +334,26 @@
                 start(side[REACH - s])
 
     c0, t0, raw = lv[0]["c"], lv[0]["t"], lv[0]["raw"]
-    msg_c = [rim_messages(n, lv[n]["c"], lv[n]["spc"], lv[n]["rpc"], RIM[n]) for n in range(3)]
+    msg_c = [rim_messages(n, lv[n]["c"], lv[n]["spc"], lv[n]["rpc"], RIM[n] - (n == 0)) for n in range(3)]
     msg_t = [
         rim_messages(
-            n, lv[n]["t"] if n > 0 else raw, lv[n]["spt"], lv[n]["rpt"], RIM[n] - 1
+            n, lv[n]["t"] if n > 0 else raw, lv[n]["spt"], lv[n]["rpt"], RIM[n] - 1 - (n == 0)
         )
         for n in range(3)
     ]
+    late = []
+    for array, reach in ((c0, RIM[0] - 1), (raw, RIM[0] - 2)):
+        rim, own, lanes = RIM[0], OX[0], pl.ds(0, 256)
+        for dx, source, target in (
+            (-1, rim + reach, rim + own + reach),
+            (1, rim + own - reach - 1, rim - reach - 1),
+        ):
+            src, dst = (array.at[pl.ds(row, 1), :, lanes] for row in (source, target))
+            late.append(message(src, dst, dx, 0))
     msg_fc, msg_ft = far_messages(far_c, side_c), far_messages(far_t, side_t)
     all_sc, msg_sc = side_messages(far_c, side_c)
     all_st, msg_st = side_messages(far_t, side_t)
-    every = sum(msg_c + msg_t, []) + msg_fc + msg_ft + all_sc + all_st
+    every = sum(msg_c + msg_t, late) + msg_fc + msg_ft + all_sc + all_st
 
     barrier = pltpu.get_barrier_semaphore()
     far_away = [d for d in range(-REACH, REACH + 1) if abs(d) > DIRECT]
@@ -472,21 +481,21 @@
             dst[i] = dst[i] + extra
             dst[i + 1] = dst[i + 1] + extra
 
-        over_rows(0, n, body, 2)
+        over_rows(0, n, body, 6)
 
     def all_coefficients(level, low, high):
         refs_c = [lv[level].get(k) for k in ("c", "e", "y4", "z", "q", "r", "g")]
         coefficients(level, *refs_c, low, high)
 
-    n0, h0 = OX[0], RIM[0] - 1
-    gather(0, "c", msg_c[0], 24, RIM[0], (0,))
+    n0, h0 = OX[0], RIM[0] - 2
+    gather(0, "c", msg_c[0], 24, h0 + 1, (0,))
     gather(0, "t", msg_t[0], 32, h0, (0,))
     all_coefficients(0, 1, n0 - 1)
-    start(msg_c[1] + msg_c[2])
+    start(msg_c[1] + late + msg_c[2])
     first_sweep(0, 1, n0 - 1)
     sweep_range(0, t0, lv[0]["a"], 2, n0 - 2)
     remainder_rows(0, lv[0]["a"], 2, OX[1] - 2)
-    gather(0, "c", msg_c[0], 24, RIM[0], (-1, 1))
+    gather(0, "c", msg_c[0], 24, h0 + 1, (-1, 1))
     gather(0, "t", msg_t[0], 32, h0, (-1, 1))
     for low, high in ((-h0, 1), (n0 - 1, n0 + h0)):
         all_coefficients(0, low, high)
@@ -506,6 +515,15 @@
         start(msg_t[level][4:] + msg_t[level][2:4])
         if level == 2:
             pass_on(msg_fc, msg_sc)
+        if level == 1:
+            arrived(late)
+            for side in (-1, 1):
+                unpack_columns(0, c0, lv[0]["rpc"], 24, h0 + 2, side, h0 + 1)
+                unpack_columns(0, raw, lv[0]["rpt"], 32, h0 + 1, side, h0)
+            for row, inward in ((-h0 - 1, -h0), (n0 + h0, n0 + h0 - 1)):
+                all_coefficients(0, row, row + 1)
+                first_sweep(0, row, row + 1)
+                sweep_range(0, t0, lv[0]["a"], inward, inward + 1)
         gather(level, "c", msg_c[level], 24, RIM[level], (0, -1, 1))
         all_coefficients(level, -h, own + h)
         gather(level, "t", msg_t[level], 32, h, (0,))
@@ -536,7 +554,7 @@
                 tile = jnp.where(lane >= 96, roll(left, 96 - 32 * k, 1), tile)
                 dest[4 * b + k] = tile if factor is None else tile * factor[4 * b + k]
 
-        over_rows(0, FAR, body, 2)
+        over_rows(0, FAR, body, FAR)
 
     for one in all_sc + all_st:
         one.pending = ["arrived", "sent"]
@@ -583,16 +601,16 @@
     sweep(0, a0, b0, 1)
     args0 = refs(0)
     stores = []
-    for part in range(2):
-        first = RIM[0] + 16 * part
-
-        over_rows(first, 16, lambda i: sweep_row(b0, a0, *args0, i), UNROLL[0])
+    for part, (low, rows) in enumerate(((0, 16), (16, 8), (24, 8))):
+        first = RIM[0] + low
+
+        over_rows(first, rows, lambda i: sweep_row(b0, a0, *args0, i), UNROLL[0])
         for n in range(2):
             for k in range(16):
                 kk = (k % 2) * 8 + k // 2
                 store = pltpu.make_async_copy(
-                    a0.at[pl.ds(first, 16), 16 * n + kk, pl.ds(0, 256)],
-                    o_ref.at[n, k, pl.ds(16 * part, 16), :],
+                    a0.at[pl.ds(first, rows), 16 * n + kk, pl.ds(0, 256)],
+                    o_ref.at[n, k, pl.ds(low, rows), :],
                     out_sem.at[32 * part + 16 * n + k],
                 )
                 store.start()
@@ -624,8 +642,8 @@
         pltpu.VMEM((32, 256), jnp.int32),
         pltpu.VMEM((32, 256), jnp.int32),
     ]
-    messages = 6 * 8 + 4 * REACH + 8 * (REACH - DIRECT) + 8
-    scratch += [pltpu.SemaphoreType.DMA((51,)), pltpu.SemaphoreType.DMA((64,))]
+    messages = 4 + 6 * 8 + 4 * REACH + 8 * (REACH - DIRECT) + 8
+    scratch += [pltpu.SemaphoreType.DMA((51,)), pltpu.SemaphoreType.DMA((96,))]
     scratch += [pltpu.SemaphoreType.DMA((messages,)), pltpu.SemaphoreType.DMA((messages,))]
 
     def per_device(misfit, viscosity, friction, ice_mask, grounded):

time: 65.3 us -> 63.9 us (0.979)
  Pallas kernels: 62.5 us -> 60.9 us
    pallas_call x1, Pallas kernels: 62.5 us -> 60.9 us  [per_device(): pl.pallas_call(functools.partial(kernel, nx, ny), out_shape=jax.ShapeDtyp...]
where the time goes in v6:
time: 63.9 us; the launch traced here: 63.2 us
  Pallas kernels  60.9 us (95%)
  local copies, waits for them, and re-layouts  2.31 us (4%)
    pallas_call x1, Pallas kernels, per_device(): pl.pallas_call(functools.partial(kernel, nx, ny), out_shape=jax.ShapeDtyp...  60.9 us
    unnamed x1, local copies, waits for them, and re-layouts  2.31 us

profile of v6, /device:TPU:5, one launch (start us, length us, event | category | flops | bytes accessed | tf_op | source)
XLA Modules:
  0.0 63.2 jit_solution(9044262014869398113)
XLA Ops:
  0.0 60.9 %shard_map.55 = f32[2,16,32,256]{3,2,1,0:T(8,128)} custom-call(f32[2,16,32,256]{3,2,1,0:T(8,128)} %m_ref.1, f32[16,32,256]{2,1,0:T(8,128)} %v_ref.1, f32[32,256]{1,0:T(8,128)} %f_ref.1, s32[32,256]{1,0:T(8,128)} %i_ref.1, s32[32,256]{1,0:T(8,128)} %b_ref.1), custom_call_target="tpu_custom_call" | custom-call | tf_op jit(solution)/shard_map/pallas_call | solution.py:650
  60.9 2.3 %copy.7 = f32[2,16,32,256]{3,2,1,0:T(8,128)} copy(f32[2,16,32,256]{3,2,1,0:T(8,128)} %shard_map.55) | data formatting | bytes 2097152

commit v7 on v6

--- a/solution.py
+++ b/solution.py
@@ -337,23 +337,28 @@
     msg_c = [rim_messages(n, lv[n]["c"], lv[n]["spc"], lv[n]["rpc"], RIM[n] - (n == 0)) for n in range(3)]
     msg_t = [
         rim_messages(
-            n, lv[n]["t"] if n > 0 else raw, lv[n]["spt"], lv[n]["rpt"], RIM[n] - 1 - (n == 0)
+            n, lv[n]["t"] if n > 0 else raw, lv[n]["spt"], lv[n]["rpt"], 2
         )
         for n in range(3)
     ]
-    late = []
-    for array, reach in ((c0, RIM[0] - 1), (raw, RIM[0] - 2)):
-        rim, own, lanes = RIM[0], OX[0], pl.ds(0, 256)
-        for dx, source, target in (
-            (-1, rim + reach, rim + own + reach),
-            (1, rim + own - reach - 1, rim - reach - 1),
-        ):
-            src, dst = (array.at[pl.ds(row, 1), :, lanes] for row in (source, target))
-            late.append(message(src, dst, dx, 0))
+    def late_messages(level, array, near, far):
+        rim, own, lanes = RIM[level], OX[level], pl.ds(0, max(OY[level], 128))
+        return [
+            message(
+                array.at[pl.ds(source, far - near), :, lanes],
+                array.at[pl.ds(target, far - near), :, lanes], dx, 0)
+            for dx, source, target in (
+                (-1, rim + near, rim + own + near),
+                (1, rim + own - far, rim - far),
+            )
+        ]
+
+    late = late_messages(0, c0, RIM[0] - 1, RIM[0]) + late_messages(0, raw, 2, RIM[0] - 1)
+    late_t = {n: late_messages(n, lv[n]["t"], 2, RIM[n] - 1) for n in (1, 2)}
     msg_fc, msg_ft = far_messages(far_c, side_c), far_messages(far_t, side_t)
     all_sc, msg_sc = side_messages(far_c, side_c)
     all_st, msg_st = side_messages(far_t, side_t)
-    every = sum(msg_c + msg_t, late) + msg_fc + msg_ft + all_sc + all_st
+    every = sum(msg_c + msg_t, late + late_t[1] + late_t[2]) + msg_fc + msg_ft + all_sc + all_st
 
     barrier = pltpu.get_barrier_semaphore()
     far_away = [d for d in range(-REACH, REACH + 1) if abs(d) > DIRECT]
@@ -425,7 +430,7 @@
             which = {0: messages[2:4], -1: messages[1:2] + messages[4:6], 1: messages[0:1] + messages[6:8]}
             arrived(which[side])
         if OY[level] < 128 and 0 in sides:
-            sent(messages[:2])
+            sent(messages[:2] + (late_t[level] if kind == "t" else []))
         for side in sides:
             unpack_columns(level, array, landed, planes, reach, side)
 
@@ -505,6 +510,16 @@
     for low, high in ((0, 2), (OX[1] - 2, OX[1])):
         remainder_rows(0, lv[0]["a"], low, high)
 
+    def outer_rows(level):
+        own, h = OX[level], RIM[level] - 1
+        arrived(late_t[level])
+        for side in (-1, 1):
+            unpack_columns(level, lv[level]["t"], lv[level]["rpt"], 32, h, side, 2)
+        for low, high in ((-h, -2), (own + 2, own + h)):
+            first_sweep(level, low, high)
+        for low, high in ((1 - h, -1), (own + 1, own + h - 1)):
+            sweep_range(level, lv[level]["t"], lv[level]["a"], low, high)
+
     for level in (1, 2):
         t, own, h = lv[level]["t"], OX[level], RIM[level] - 1
         if level == 2:
@@ -512,8 +527,9 @@
         t[RIM[level] : RIM[level] + own, :, 0:128] = restricted(level - 1)
         start(msg_t[level][:2])
         pack_columns(level, t, lv[level]["spt"], 32)
-        start(msg_t[level][4:] + msg_t[level][2:4])
+        start(msg_t[level][4:] + msg_t[level][2:4] + late_t[level])
         if level == 2:
+            outer_rows(1)
             pass_on(msg_fc, msg_sc)
         if level == 1:
             arrived(late)
@@ -526,22 +542,23 @@
                 sweep_range(0, t0, lv[0]["a"], inward, inward + 1)
         gather(level, "c", msg_c[level], 24, RIM[level], (0, -1, 1))
         all_coefficients(level, -h, own + h)
-        gather(level, "t", msg_t[level], 32, h, (0,))
+        gather(level, "t", msg_t[level], 32, 2, (0,))
         if OY[level] >= 128:
-            sent(msg_t[level][:2])
+            sent(msg_t[level][:2] + late_t[level])
             start(msg_fc + msg_sc[REACH])
         first_sweep(level, 0, own)
         sweep_range(level, t, lv[level]["a"], 1, own - 1)
-        gather(level, "t", msg_t[level], 32, h, (-1, 1))
-        first_sweep(level, -h, 0)
-        first_sweep(level, own, own + h)
-        sweep_range(level, t, lv[level]["a"], 1 - h, 1)
-        sweep_range(level, t, lv[level]["a"], own - 1, own + h - 1)
+        gather(level, "t", msg_t[level], 32, 2, (-1, 1))
+        first_sweep(level, -2, 0)
+        first_sweep(level, own, own + 2)
+        sweep_range(level, t, lv[level]["a"], -1, 1)
+        sweep_range(level, t, lv[level]["a"], own - 1, own + 1)
 
     remainder_rows(2, lv[2]["a"], 0, OX[3])
     t_next = restricted(2)
     far_t[REACH] = sum(roll(t_next[k], 32 * k, 1) for k in range(4))
     start(msg_ft + msg_st[REACH])
+    outer_rows(2)
 
     def unpack_far(dest, far, side, planes, factor):
         lane = lane_iota(planes)
@@ -642,7 +659,7 @@
         pltpu.VMEM((32, 256), jnp.int32),
         pltpu.VMEM((32, 256), jnp.int32),
     ]
-    messages = 4 + 6 * 8 + 4 * REACH + 8 * (REACH - DIRECT) + 8
+    messages = 8 + 6 * 8 + 4 * REACH + 8 * (REACH - DIRECT) + 8
     scratch += [pltpu.SemaphoreType.DMA((51,)), pltpu.SemaphoreType.DMA((96,))]
     scratch += [pltpu.SemaphoreType.DMA((messages,)), pltpu.SemaphoreType.DMA((messages,))]
 

time: 63.9 us -> 62.2 us (0.973)
  Pallas kernels: 60.9 us -> 59.3 us
    pallas_call x1, Pallas kernels: 60.9 us -> 59.3 us  [per_device(): pl.pallas_call(functools.partial(kernel, nx, ny), out_shape=jax.ShapeDtyp...]
where the time goes in v7:
time: 62.2 us; the launch traced here: 61.6 us
  Pallas kernels  59.3 us (95%)
  local copies, waits for them, and re-layouts  2.31 us (4%)
    pallas_call x1, Pallas kernels, per_device(): pl.pallas_call(functools.partial(kernel, nx, ny), out_shape=jax.ShapeDtyp...  59.3 us
    unnamed x1, local copies, waits for them, and re-layouts  2.31 us

profile of v7, /device:TPU:5, one launch (start us, length us, event | category | flops | bytes accessed | tf_op | source)
XLA Modules:
  0.0 61.6 jit_solution(9159515360977010127)
XLA Ops:
  0.0 59.3 %shard_map.55 = f32[2,16,32,256]{3,2,1,0:T(8,128)} custom-call(f32[2,16,32,256]{3,2,1,0:T(8,128)} %m_ref.1, f32[16,32,256]{2,1,0:T(8,128)} %v_ref.1, f32[32,256]{1,0:T(8,128)} %f_ref.1, s32[32,256]{1,0:T(8,128)} %i_ref.1, s32[32,256]{1,0:T(8,128)} %b_ref.1), custom_call_target="tpu_custom_call" | custom-call | tf_op jit(solution)/shard_map/pallas_call | solution.py:667
  59.3 2.3 %copy.7 = f32[2,16,32,256]{3,2,1,0:T(8,128)} copy(f32[2,16,32,256]{3,2,1,0:T(8,128)} %shard_map.55) | data formatting | bytes 2097152

commit v8 on v7

--- a/solution.py
+++ b/solution.py
@@ -19,7 +19,7 @@
 RIM = (4, 5, 6, 24)
 PW = (4, 8, 16, 32)
 TX = tuple(o + 2 * h for o, h in zip(OX[:3], RIM)) + (64,)
-UNROLL = (4, 6, 8, 16)
+UNROLL = (4, 10, 9, 16)
 UNROLL_C = (4, 4, 6, 10)
 UNROLL_R = (2, 4, 4)
 DIRECT = 6
@@ -382,17 +382,17 @@
     loads = []
     for k in range(16):
         kk = (k % 2) * 8 + k // 2
-        loads.append((v_ref.at[k], lv[0]["c"].at[own0, kk, pl.ds(0, 256)]))
+        loads.append((v_ref.at[k], c0.at[own0, kk, pl.ds(0, 256)], 0))
         for n in range(2):
-            loads.append((m_ref.at[n, k], raw.at[own0, 16 * n + kk, pl.ds(0, 256)]))
-    loads += [(f_ref, fr), (i_ref, ic), (b_ref, gr)]
-    loads = [pltpu.make_async_copy(s, d, in_sem.at[n]) for n, (s, d) in enumerate(loads)]
-    for load in loads:
-        load.start()
+            loads.append((m_ref.at[n, k], raw.at[own0, 16 * n + kk, pl.ds(0, 256)], 1))
+    loads += [(f_ref, fr, 2), (i_ref, ic, 3), (b_ref, gr, 4)]
+    for source, target, n in loads:
+        pltpu.make_async_copy(source, target, in_sem.at[n]).start()
+    landed = [c0.at[own0, pl.ds(0, 16), pl.ds(0, 256)], raw.at[own0, :, pl.ds(0, 256)], fr, ic, gr]
 
     clear(every)
-    for load in loads:
-        load.wait()
+    for n, target in enumerate(landed):
+        pltpu.make_async_copy(target, target, in_sem.at[n]).wait()
 
     ic_f = ic[...].astype(jnp.float32)
     ic_f = ic_f.reshape(OX[0], 1, 256)
@@ -628,10 +628,11 @@
                 store = pltpu.make_async_copy(
                     a0.at[pl.ds(first, rows), 16 * n + kk, pl.ds(0, 256)],
                     o_ref.at[n, k, pl.ds(low, rows), :],
-                    out_sem.at[32 * part + 16 * n + k],
+                    out_sem.at[part],
                 )
                 store.start()
-                stores.append(store)
+        done = a0.at[pl.ds(first, rows), :, pl.ds(0, 256)]
+        stores.append(pltpu.make_async_copy(done, done, out_sem.at[part]))
     sent([one for one in every if one.pending])
     for store in stores:
         store.wait()
@@ -660,7 +661,7 @@
         pltpu.VMEM((32, 256), jnp.int32),
     ]
     messages = 8 + 6 * 8 + 4 * REACH + 8 * (REACH - DIRECT) + 8
-    scratch += [pltpu.SemaphoreType.DMA((51,)), pltpu.SemaphoreType.DMA((96,))]
+    scratch += [pltpu.SemaphoreType.DMA((5,)), pltpu.SemaphoreType.DMA((3,))]
     scratch += [pltpu.SemaphoreType.DMA((messages,)), pltpu.SemaphoreType.DMA((messages,))]
 
     def per_device(misfit, viscosity, friction, ice_mask, grounded):

time: 62.2 us -> 60.6 us (0.974)
  Pallas kernels: 59.3 us -> 57.8 us
    pallas_call x1, Pallas kernels: 59.3 us -> 57.8 us  [per_device(): pl.pallas_call(functools.partial(kernel, nx, ny), out_shape=jax.ShapeDtyp...]
where the time goes in v8:
time: 60.6 us; the launch traced here: 60.1 us
  Pallas kernels  57.8 us (95%)
  local copies, waits for them, and re-layouts  2.31 us (4%)
    pallas_call x1, Pallas kernels, per_device(): pl.pallas_call(functools.partial(kernel, nx, ny), out_shape=jax.ShapeDtyp...  57.8 us
    unnamed x1, local copies, waits for them, and re-layouts  2.31 us

profile of v8, /device:TPU:5, one launch (start us, length us, event | category | flops | bytes accessed | tf_op | source)
XLA Modules:
  0.0 60.1 jit_solution(10753955170598592802)
XLA Ops:
  0.0 57.8 %shard_map.55 = f32[2,16,32,256]{3,2,1,0:T(8,128)} custom-call(f32[2,16,32,256]{3,2,1,0:T(8,128)} %m_ref.1, f32[16,32,256]{2,1,0:T(8,128)} %v_ref.1, f32[32,256]{1,0:T(8,128)} %f_ref.1, s32[32,256]{1,0:T(8,128)} %i_ref.1, s32[32,256]{1,0:T(8,128)} %b_ref.1), custom_call_target="tpu_custom_call" | custom-call | tf_op jit(solution)/shard_map/pallas_call | solution.py:668
  57.8 2.3 %copy.7 = f32[2,16,32,256]{3,2,1,0:T(8,128)} copy(f32[2,16,32,256]{3,2,1,0:T(8,128)} %shard_map.55) | data formatting | bytes 2097152

commit v9 on v8

--- a/solution.py
+++ b/solution.py
@@ -19,7 +19,7 @@
 RIM = (4, 5, 6, 24)
 PW = (4, 8, 16, 32)
 TX = tuple(o + 2 * h for o, h in zip(OX[:3], RIM)) + (64,)
-UNROLL = (4, 10, 9, 16)
+UNROLL = (8, 10, 9, 16)
 UNROLL_C = (4, 4, 6, 10)
 UNROLL_R = (2, 4, 4)
 DIRECT = 6
@@ -618,7 +618,7 @@
     sweep(0, a0, b0, 1)
     args0 = refs(0)
     stores = []
-    for part, (low, rows) in enumerate(((0, 16), (16, 8), (24, 8))):
+    for part, (low, rows) in enumerate(((0, 24), (24, 8))):
         first = RIM[0] + low
 
         over_rows(first, rows, lambda i: sweep_row(b0, a0, *args0, i), UNROLL[0])

time: 60.6 us -> 60.4 us (level)
  no operation moved by 1% of the time
where the time goes in v9:
time: 60.4 us; the launch traced here: 59.8 us
  Pallas kernels  57.5 us (95%)
  local copies, waits for them, and re-layouts  2.31 us (4%)
    pallas_call x1, Pallas kernels, per_device(): pl.pallas_call(functools.partial(kernel, nx, ny), out_shape=jax.ShapeDtyp...  57.5 us
    unnamed x1, local copies, waits for them, and re-layouts  2.31 us

profile of v9, /device:TPU:5, one launch (start us, length us, event | category | flops | bytes accessed | tf_op | source)
XLA Modules:
  0.0 59.8 jit_solution(7816236995938903561)
XLA Ops:
  0.0 57.5 %shard_map.55 = f32[2,16,32,256]{3,2,1,0:T(8,128)} custom-call(f32[2,16,32,256]{3,2,1,0:T(8,128)} %m_ref.1, f32[16,32,256]{2,1,0:T(8,128)} %v_ref.1, f32[32,256]{1,0:T(8,128)} %f_ref.1, s32[32,256]{1,0:T(8,128)} %i_ref.1, s32[32,256]{1,0:T(8,128)} %b_ref.1), custom_call_target="tpu_custom_call" | custom-call | tf_op jit(solution)/shard_map/pallas_call | solution.py:668
  57.5 2.3 %copy.7 = f32[2,16,32,256]{3,2,1,0:T(8,128)} copy(f32[2,16,32,256]{3,2,1,0:T(8,128)} %shard_map.55) | data formatting | bytes 2097152
